TPU v7x, 256 devices: a whole 4x4x8 slice. The times are simulated.
256 devices in a mesh: section: 2 (over z_hi), grp: 16 (over z_lo, y), sta: 8 (over x, core).
Axes of the slice: x: 4, y: 4, z: 8 (z_hi: 2, z_lo: 4; z = z_hi * 4 + z_lo), core: 2. Of those that a mesh axis runs over, the one named last changes fastest.
Arguments:
- records: bfloat16 [512, 4, 3, 16384], P(('section', 'grp', 'sta')), may hold values from -6 to 6
- fir_taps: float32 [64], replicated, may hold values from -0.75 to 0.75
- band_bins: int32 [4, 2], replicated, may hold values from 0 to 2048, as said below
- station_live: int32 [512], P(('section', 'grp', 'sta')), may hold values 0 or 1
- block_live: int32 [64], P(('section', 'grp')), may hold values 0 or 1
Outputs:
- correlations: float32 [2304, 64, 1024], P('sta', ('section', 'grp'))
Inputs may be any that keep to these rules, and one draw needn't show every extreme that they name: band_bins[b, 0] < band_bins[b, 1]; each band spans 64 to 256 bins.
All inputs are finite; a program needn't handle non-finite values. No bound on the sum of `station_live` or of `block_live` on one device may be relied on, other than what follows from the above.
Results may differ from a plain program's by a relative error of at most 0.0077.
Values may be sent and summed in bfloat16 or wider, within the bound.
A program may use at most 64 MiB of HBM per device.

v0:
```python
import math

import jax
import jax.numpy as jnp
from jax import lax
from jax.sharding import PartitionSpec as P

BINS = 2048
NT = 4096
DEC = 4
TAPS = 64
OFFS = 2
LAGS = 1024


epsilon = 1e-06


def passed_along(block, axis, distance):
    devices = range(lax.axis_size(axis))
    route = [((i - distance) % len(devices), i) for i in devices]
    return lax.ppermute(block, axis, route)


def band_matrix(fir_taps, frames, offset):
    span = DEC * frames
    position = jnp.arange(span, dtype=jnp.int32)[:, None]
    output = jnp.arange(frames, dtype=jnp.int32)[None, :]
    tap_index = DEC * output + offset - position
    usable = (tap_index >= 0) & (tap_index < TAPS)
    return jnp.where(usable, fir_taps[jnp.clip(tap_index, 0, TAPS - 1)], 0.0)


def decimate(recorded, fir_taps):
    leading = recorded.shape[:-1]
    frames = min(NT, 128)
    span = DEC * frames
    block_count = NT // frames
    signal = recorded.astype(jnp.float32).reshape(-1, block_count, span)
    previous = jnp.pad(signal[:, :-1], ((0, 0), (1, 0), (0, 0)))
    current_part = jnp.dot(
        signal.reshape(-1, span), band_matrix(fir_taps, frames, 0), precision=lax.Precision.HIGHEST
    )
    previous_part = jnp.dot(
        previous.reshape(-1, span),
        band_matrix(fir_taps, frames, span),
        precision=lax.Precision.HIGHEST,
    )
    summed = current_part + previous_part
    return summed.reshape(leading + (NT,)).astype(jnp.bfloat16)


def dft_table(starts, block_width):
    samples = jnp.arange(NT, dtype=jnp.int32)[:, None]
    bin_index = starts + jnp.arange(block_width, dtype=jnp.int32)[None, :]
    angles = 2.0 * math.pi / NT * (samples * bin_index % NT).astype(jnp.float32)
    return jnp.concatenate([jnp.cos(angles), -jnp.sin(angles)], axis=1).astype(jnp.bfloat16)


def spectrum(flattened):
    block_width = min(BINS, 256)

    def spectrum_advance(loop_step, buffers):
        real_part, imag_part = buffers
        starts = loop_step * block_width
        product = jnp.dot(
            flattened, dft_table(starts, block_width), preferred_element_type=jnp.float32
        )
        real_part = lax.dynamic_update_slice_in_dim(real_part, product[:, :block_width], starts, 1)
        imag_part = lax.dynamic_update_slice_in_dim(imag_part, product[:, block_width:], starts, 1)
        return (real_part, imag_part)

    empty_buffer = jnp.zeros((flattened.shape[0], BINS), jnp.float32)
    return lax.fori_loop(0, BINS // block_width, spectrum_advance, (empty_buffer, empty_buffer))


def whiten(real_part, imag_part, band_bins, station_live):
    bin_index = jnp.arange(BINS, dtype=jnp.int32)[None, :]
    inside = ((bin_index >= band_bins[:, 0:1]) & (bin_index < band_bins[:, 1:2])).astype(
        jnp.float32
    )
    band_width = (band_bins[:, 1] - band_bins[:, 0]).astype(jnp.float32)
    powers = (real_part * real_part + imag_part * imag_part).reshape(-1, BINS)
    energy = jnp.dot(powers, inside.T, precision=lax.Precision.HIGHEST) / band_width
    gains = jnp.dot(lax.rsqrt(energy + epsilon), inside, precision=lax.Precision.HIGHEST)
    gains = gains.reshape(real_part.shape) * station_live.astype(jnp.float32)[:, None, None, None]
    return jnp.concatenate([real_part * gains, imag_part * gains], axis=2).astype(jnp.bfloat16)


def cross_spectra(local_group, remote_group):
    local_swap = jnp.swapaxes(local_group, 1, 2)
    remote_swap = jnp.swapaxes(remote_group, 1, 2)
    local_re = local_swap[:, :3, None, None].astype(jnp.float32)
    local_im = local_swap[:, 3:, None, None].astype(jnp.float32)
    remote_re = remote_swap[None, None, :, :3].astype(jnp.float32)
    remote_im = remote_swap[None, None, :, 3:].astype(jnp.float32)
    real_sum = jnp.sum(local_re * remote_re + local_im * remote_im, axis=4)
    imag_sum = jnp.sum(local_im * remote_re - local_re * remote_im, axis=4)
    row_count = local_group.shape[0] * 9 * remote_group.shape[0]
    return jnp.concatenate(
        [real_sum.reshape(row_count, -1), imag_sum.reshape(row_count, -1)], axis=1
    ).astype(jnp.bfloat16)


def lag_table(frequency, parity, starts, block_width):
    lag_index = starts + jnp.arange(block_width, dtype=jnp.int32)[None, :] - LAGS // 2
    angles = 2.0 * math.pi / NT * (frequency[:, None] * lag_index % NT).astype(jnp.float32)
    weight = jnp.where(frequency == 0, 0.5, 1.0) / math.sqrt(BINS)
    values = jnp.where(parity[:, None] == 0, jnp.cos(angles), -jnp.sin(angles)) * weight[:, None]
    return values.astype(jnp.bfloat16)


def inverse(spectra, frequency, parity, kept_blocks):
    row_count, block_count, depth = spectra.shape
    flattened = spectra.reshape(row_count * block_count, depth)
    block_width = min(LAGS, 256)

    def inverse_advance(loop_step, result):
        starts = loop_step * block_width
        product = jnp.dot(
            flattened,
            lag_table(frequency, parity, starts, block_width),
            preferred_element_type=jnp.float32,
        )
        return lax.dynamic_update_slice_in_dim(result, product, starts, 1)

    result = lax.fori_loop(
        0,
        LAGS // block_width,
        inverse_advance,
        jnp.zeros((row_count * block_count, LAGS), jnp.float32),
    )
    return result.reshape(row_count, block_count, LAGS) * kept_blocks[None, :, None]


def body(records, fir_taps, band_bins, station_live, block_live):
    decimated = decimate(records, fir_taps)
    real_part, imag_part = spectrum(decimated.reshape(-1, NT))
    out_shape = decimated.shape[:-1] + (BINS,)
    local_spectra = whiten(
        real_part.reshape(out_shape), imag_part.reshape(out_shape), band_bins, station_live
    )
    kept_blocks = block_live.astype(jnp.float32)
    gathered = lax.all_gather(local_spectra, "sta", axis=0, tiled=True)
    remote = gathered
    pieces = []
    for distance in range(OFFS):
        remote = passed_along(remote, ("section", "grp"), 1)
        pieces.append(cross_spectra(local_spectra, remote))
    arrived = jnp.stack(pieces, axis=1)
    positions = jnp.arange(2 * BINS, dtype=jnp.int32)
    frequency = positions % BINS
    parity = positions // BINS
    return inverse(arrived, frequency, parity, kept_blocks)


def solution(mesh):
    in_specs = (
        P(("section", "grp", "sta"), None, None, None),
        P(),
        P(),
        P(("section", "grp", "sta")),
        P(("section", "grp")),
    )
    out_specs = P("sta", ("section", "grp"), None)
    return jax.shard_map(body, mesh=mesh, in_specs=in_specs, out_specs=out_specs, check_vma=False)
```

profile of v0, /device:TPU:1, one launch (start us, length us, event | category | flops | bytes accessed | tf_op | source)
XLA Modules:
  0.0 521.3 jit_solution(13341538282745472804)
XLA Ops:
  6.5 2.1 fusion.920
  8.6 2.1 fusion.922
  10.7 2.1 fusion.921
  12.8 1.6 fusion.923
  14.4 1.8 copy.64
  16.2 1.1 reshape.242
  17.3 1.1 reshape_reshape.3
  18.8 41.9 %fusion.86 = f32[768,128]{0,1:T(8,128)S(1)} fusion(bf16[768,512]{1,0:T(8,128)(2,1)S(1)} %bitcast.764, f32[]{:T(128)} %bitcast.115, f32[]{:T(128)} %bitcast.116, f32[]{:T(128)} %bitcast.117, f32[]{:T(128)} %bitcast.118, f32[]{:T(128)} %bitcast.119, f32[]{:T(128)} %bitcast.121, f32[]{:T(128)} %bitcast.120, f32[]{:T(128)} %bitcast.2, f32[]{:T(128)} %bitcast.4, ...), kind=kOutput, calls=%fused_computation.119 | convolution fusion | flops 612892672 | bytes 1180416 | tf_op jit(solution)/shard_map/dot_general | solution.py:44
  60.7 41.9 %fusion.45 = bf16[768,128]{0,1:T(8,128)(2,1)S(1)} fusion(f32[768,128]{0,1:T(8,128)S(1)} %fusion.86, bf16[768,512]{1,0:T(8,128)(2,1)S(1)} %reshape_reshape.3, f32[]{:T(128)} %bitcast.115, f32[]{:T(128)} %bitcast.116, f32[]{:T(128)} %bitcast.117, f32[]{:T(128)} %bitcast.118, f32[]{:T(128)} %bitcast.119, f32[]{:T(128)} %bitcast.121, f32[]{:T(128)} %bitcast.120, ...), kind=kOutput, calls=%fused_computation.68 | convolution fusion | flops 613089280 | bytes 1377024 | tf_op jit(solution)/shard_map/dot_general | solution.py:41
  102.9 141.6 %while.34 = (s32[]{:T(128)}, f32[24,2048]{1,0:T(8,128)S(1)}, f32[24,2048]{1,0:T(8,128)S(1)}, bf16[24,4096]{1,0:T(8,128)(2,1)S(1)}, s32[]{:T(128)}, /*index=5*/s32[]{:T(128)}, s32[]{:T(128)}, s32[]{:T(128)}) while((s32[]{:T(128)}, f32[24,2048]{1,0:T(8,128)S(1)}, f32[24,2048]{1,0:T(8,128)S(1)}, bf16[24,4096]{1,0:T(8,128)(2,1)S(1)}, s32[]{:T(128)}, ...), condition=%wide.region_1.2_spmd, body=%wide.region_0.1_spmd.sunk | while | flops 126877952 | bytes 8734859 | solution.py:74
  103.0 17.0 %cosine_convert_fusion.2 = (bf16[4096,256]{1,0:T(8,128)(2,1)S(1)}, bf16[4096,256]{1,0:T(8,128)(2,1)S(1)}) fusion(s32[256]{0:T(256)S(1)} %iota_add_fusion.2), kind=kLoop, calls=%fused_computation.13.clone.1 | loop fusion | flops 17825792 | bytes 4195328 | tf_op jit(solution)/shard_map/convert
  119.9 0.7 fusion.943
  120.7 17.0 %cosine_convert_fusion.2 = (bf16[4096,256]{1,0:T(8,128)(2,1)S(1)}, bf16[4096,256]{1,0:T(8,128)(2,1)S(1)}) fusion(s32[256]{0:T(256)S(1)} %iota_add_fusion.2), kind=kLoop, calls=%fused_computation.13.clone.1 | loop fusion | flops 17825792 | bytes 4195328 | tf_op jit(solution)/shard_map/convert
  137.6 0.7 fusion.943
  138.4 17.0 %cosine_convert_fusion.2 = (bf16[4096,256]{1,0:T(8,128)(2,1)S(1)}, bf16[4096,256]{1,0:T(8,128)(2,1)S(1)}) fusion(s32[256]{0:T(256)S(1)} %iota_add_fusion.2), kind=kLoop, calls=%fused_computation.13.clone.1 | loop fusion | flops 17825792 | bytes 4195328 | tf_op jit(solution)/shard_map/convert
  156.1 17.0 %cosine_convert_fusion.2 = (bf16[4096,256]{1,0:T(8,128)(2,1)S(1)}, bf16[4096,256]{1,0:T(8,128)(2,1)S(1)}) fusion(s32[256]{0:T(256)S(1)} %iota_add_fusion.2), kind=kLoop, calls=%fused_computation.13.clone.1 | loop fusion | flops 17825792 | bytes 4195328 | tf_op jit(solution)/shard_map/convert
  173.7 17.0 %cosine_convert_fusion.2 = (bf16[4096,256]{1,0:T(8,128)(2,1)S(1)}, bf16[4096,256]{1,0:T(8,128)(2,1)S(1)}) fusion(s32[256]{0:T(256)S(1)} %iota_add_fusion.2), kind=kLoop, calls=%fused_computation.13.clone.1 | loop fusion | flops 17825792 | bytes 4195328 | tf_op jit(solution)/shard_map/convert
  191.4 17.0 %cosine_convert_fusion.2 = (bf16[4096,256]{1,0:T(8,128)(2,1)S(1)}, bf16[4096,256]{1,0:T(8,128)(2,1)S(1)}) fusion(s32[256]{0:T(256)S(1)} %iota_add_fusion.2), kind=kLoop, calls=%fused_computation.13.clone.1 | loop fusion | flops 17825792 | bytes 4195328 | tf_op jit(solution)/shard_map/convert
  208.4 0.7 fusion.943
  209.1 17.0 %cosine_convert_fusion.2 = (bf16[4096,256]{1,0:T(8,128)(2,1)S(1)}, bf16[4096,256]{1,0:T(8,128)(2,1)S(1)}) fusion(s32[256]{0:T(256)S(1)} %iota_add_fusion.2), kind=kLoop, calls=%fused_computation.13.clone.1 | loop fusion | flops 17825792 | bytes 4195328 | tf_op jit(solution)/shard_map/convert
  226.1 0.7 fusion.943
  226.8 17.0 %cosine_convert_fusion.2 = (bf16[4096,256]{1,0:T(8,128)(2,1)S(1)}, bf16[4096,256]{1,0:T(8,128)(2,1)S(1)}) fusion(s32[256]{0:T(256)S(1)} %iota_add_fusion.2), kind=kLoop, calls=%fused_computation.13.clone.1 | loop fusion | flops 17825792 | bytes 4195328 | tf_op jit(solution)/shard_map/convert
  243.8 0.7 fusion.943
  245.8 0.8 fusion.919
  246.6 31.2 %all-gather.2.cloned.1.call-done = bf16[16,4,6,2048]{3,1,2,0:T(4,128)(2,1)} async-done(((bf16[2,4,6,2048]{3,1,2,0:T(4,128)(2,1)}), bf16[16,4,6,2048]{3,1,2,0:T(4,128)(2,1)}) %all-gather.2.cloned.1.call-update) | async-done | bytes 1572880 | tf_op jit(solution)/shard_map/all_gather | solution.py:144
  277.9 2.3 copy.71
  280.1 1.5 collective-permute-start
  281.6 38.6 %collective-permute-done = bf16[16,4,6,2048]{3,0,2,1:T(8,128)(2,1)S(1)} collective-permute-done((bf16[16,4,6,2048]{3,0,2,1:T(8,128)(2,1)S(1)}, bf16[16,4,6,2048]{3,0,2,1:T(8,128)(2,1)S(1)}, u32[]{:S(2)}, u32[]{:S(2)}) %collective-permute-start) | collective-permute-done | bytes 1572896 | tf_op jit(solution)/shard_map/ppermute | solution.py:22
  320.6 38.1 %collective-permute-done.1 = bf16[16,4,6,2048]{3,0,2,1:T(8,128)(2,1)S(1)} collective-permute-done((bf16[16,4,6,2048]{3,0,2,1:T(8,128)(2,1)S(1)}, bf16[16,4,6,2048]{3,0,2,1:T(8,128)(2,1)S(1)}, u32[]{:S(2)}, u32[]{:S(2)}) %collective-permute-start.1) | collective-permute-done | bytes 1572896 | tf_op jit(solution)/shard_map/ppermute | solution.py:22
  359.1 13.0 %add_reduce_fusion.1 = (bf16[2,3,16,3,2048]{4,2,3,1,0:T(8,128)(2,1)S(1)}, bf16[2,3,16,3,2048]{4,2,3,1,0:T(8,128)(2,1)}, bf16[2,3,16,3,2048]{4,2,3,1,0:T(8,128)(2,1)}, bf16[2,3,16,3,2048]{4,2,3,1,0:T(8,128)(2,1)}) fusion(f32[2,3,4,2048]{3,2,1,0:T(4,128)S(1)} %get-tuple-element.311, f32[2,3,4,2048]{3,2,1,0:T(4,128)S(1)} %get-tuple-element.310, ...), kind=kLoop, calls=%fused_computation.63 | loop fusion | flops 35389440 | bytes 11403264 | tf_op jit(solution)/shard_map/reduce_sum | solution.py:97
  372.1 1.0 copy.74
  373.1 1.0 concatenate.46
  374.1 2.3 copy.75
  376.5 2.2 concatenate.47
  378.7 2.3 copy.78
  381.0 2.2 concatenate.49
  383.2 2.3 copy.79
  385.5 2.2 concatenate.50
  387.7 4.8 maximum_maximum_fusion
  392.5 9.5 %copy.80 = bf16[288,2,4096]{2,1,0:T(2,128)(2,1)} copy(bf16[288,2,4096]{2,0,1:T(8,128)(2,1)} %maximum_maximum_fusion) | data formatting | bytes 9437184 | tf_op jit(solution)/shard_map/stack | solution.py:150
  402.0 8.0 %reshape.248 = bf16[576,4096]{1,0:T(8,128)(2,1)} reshape(bf16[288,2,4096]{2,1,0:T(2,128)(2,1)} %copy.80) | data formatting | bytes 9437184 | tf_op jit(solution)/shard_map/reshape | solution.py:115
  410.3 97.7 %while.35 = (s32[]{:T(128)}, f32[576,1024]{1,0:T(8,128)S(1)}, bf16[576,4096]{1,0:T(8,128)(2,1)}, s32[]{:T(128)}, s32[]{:T(128)}, /*index=5*/s32[]{:T(128)}, s32[]{:T(128)}) while((s32[]{:T(128)}, f32[576,1024]{1,0:T(8,128)S(1)}, bf16[576,4096]{1,0:T(8,128)(2,1)}, s32[]{:T(128)}, s32[]{:T(128)}, /*index=5*/s32[]{:T(128)}, ...), condition=%wide.region_7.8_spmd.clone.clone, body=%wide.region_6.7_spmd.clone.clone.sunk | while | flops 1226932736 | bytes 5384323 | solution.py:127
  410.4 24.3 %fusion.947 = f32[576,1024]{1,0:T(8,128)S(1)} fusion(f32[576,1024]{1,0:T(8,128)S(1)} %get-tuple-element.464, s32[]{:T(128)S(6)} %select_n.1065, bf16[576,4096]{1,0:T(8,128)(2,1)} %get-tuple-element.472, f32[4096]{0:T(1024)S(1)} %select_multiply_fusion.2, s32[256]{0:T(256)S(1)} %add_add_fusion.2, s32[4096]{0:T(1024)S(1)} %fusion.945, ...), kind=kOutput, calls=%fused_computation.41.clone.2 | convolution fusion | flops 1226833920 | bytes 5346308 | tf_op jit(solution)/shard_map/while/body/eval_jaxpr/dot_general | solution.py:120
  434.8 24.3 %fusion.947 = f32[576,1024]{1,0:T(8,128)S(1)} fusion(f32[576,1024]{1,0:T(8,128)S(1)} %get-tuple-element.464, s32[]{:T(128)S(6)} %select_n.1065, bf16[576,4096]{1,0:T(8,128)(2,1)} %get-tuple-element.472, f32[4096]{0:T(1024)S(1)} %select_multiply_fusion.2, s32[256]{0:T(256)S(1)} %add_add_fusion.2, s32[4096]{0:T(1024)S(1)} %fusion.945, ...), kind=kOutput, calls=%fused_computation.41.clone.2 | convolution fusion | flops 1226833920 | bytes 5346308 | tf_op jit(solution)/shard_map/while/body/eval_jaxpr/dot_general | solution.py:120
  459.2 24.4 %fusion.947 = f32[576,1024]{1,0:T(8,128)S(1)} fusion(f32[576,1024]{1,0:T(8,128)S(1)} %get-tuple-element.464, s32[]{:T(128)S(6)} %select_n.1065, bf16[576,4096]{1,0:T(8,128)(2,1)} %get-tuple-element.472, f32[4096]{0:T(1024)S(1)} %select_multiply_fusion.2, s32[256]{0:T(256)S(1)} %add_add_fusion.2, s32[4096]{0:T(1024)S(1)} %fusion.945, ...), kind=kOutput, calls=%fused_computation.41.clone.2 | convolution fusion | flops 1226833920 | bytes 5346308 | tf_op jit(solution)/shard_map/while/body/eval_jaxpr/dot_general | solution.py:120
  483.6 24.4 %fusion.947 = f32[576,1024]{1,0:T(8,128)S(1)} fusion(f32[576,1024]{1,0:T(8,128)S(1)} %get-tuple-element.464, s32[]{:T(128)S(6)} %select_n.1065, bf16[576,4096]{1,0:T(8,128)(2,1)} %get-tuple-element.472, f32[4096]{0:T(1024)S(1)} %select_multiply_fusion.2, s32[256]{0:T(256)S(1)} %add_add_fusion.2, s32[4096]{0:T(1024)S(1)} %fusion.945, ...), kind=kOutput, calls=%fused_computation.41.clone.2 | convolution fusion | flops 1226833920 | bytes 5346308 | tf_op jit(solution)/shard_map/while/body/eval_jaxpr/dot_general | solution.py:120
  508.0 2.4 reshape.249
  510.5 3.9 broadcast_multiply_fusion
  (65 shorter events, 5.1 us)
Async XLA Ops:
  6.5 11.9 %copy-start = (s32[4,2]{0,1:T(2,128)S(1)}, s32[4,2]{0,1:T(2,128)}, u32[]{:S(2)}) copy-start(s32[4,2]{0,1:T(2,128)} %param.11) | copy-start | bytes 100
  6.5 271.3 %all-gather.2.cloned.1.call-start = ((), (), s32[]{:S(2)}) async-start(), calls=%async_computation | async-start | bytes 1769472 | tf_op jit(solution)/shard_map/all_gather | solution.py:144
  102.9 142.5 %copy-start.1 = (s32[2]{0:T(128)S(1)}, s32[2]{0:T(128)}, u32[]{:S(2)}) copy-start(s32[2]{0:T(128)} %param.12) | copy-start | bytes 28
  244.5 75.7 %copy-start.2 = (s32[2]{0:T(128)S(1)}, s32[2]{0:T(128)}, u32[]{:S(2)}) copy-start(s32[2]{0:T(128)} %param.13) | copy-start | bytes 28
  280.1 40.1 %collective-permute-start = (bf16[16,4,6,2048]{3,0,2,1:T(8,128)(2,1)S(1)}, bf16[16,4,6,2048]{3,0,2,1:T(8,128)(2,1)S(1)}, u32[]{:S(2)}, u32[]{:S(2)}) collective-permute-start(bf16[16,4,6,2048]{3,0,2,1:T(8,128)(2,1)S(1)} %copy.71), channel_id=1, source_target_pairs={{248,0},{0,8},{8,16},{16,24},{24,32},{32,40},{40,48},{48,56},{56,6... | collective-permute-start | bytes 4718600 | tf_op jit(solution)/shard_map/ppermute | solution.py:22
  320.2 38.5 %collective-permute-start.1 = (bf16[16,4,6,2048]{3,0,2,1:T(8,128)(2,1)S(1)}, bf16[16,4,6,2048]{3,0,2,1:T(8,128)(2,1)S(1)}, u32[]{:S(2)}, u32[]{:S(2)}) collective-permute-start(bf16[16,4,6,2048]{3,0,2,1:T(8,128)(2,1)S(1)} %collective-permute-done), channel_id=1, source_target_pairs={{248,0},{0,8},{8,16},{16,24},{24,32},{32,40},{40,48},{48,56},{56,6... | collective-permute-start | bytes 4718600 | tf_op jit(solution)/shard_map/ppermute | solution.py:22
Sparse Core Ops, SparseCore 0:
  246.8 31.0 all-gather.1
where the time goes:
time: 523 us; the launch traced here: 521 us
  matrix products  187 us (36%)
  other arithmetic  160 us (31%)
  waiting for transfers between devices  108 us (21%)
  local copies, waits for them, and re-layouts  50.9 us (10%)
  between operations  13.7 us (3%)
    another operation x9, other arithmetic  136 us
    dot_general x4, matrix products, inverse_advance(): jnp.dot(flattened, lag_table(frequency, parity, starts, block_width), pre...  97.4 us
    ppermute x2, waiting for transfers between devices, passed_along(): return lax.ppermute(block, axis, route)  76.7 us
    dot_general x1, matrix products, decimate(): jnp.dot(previous.reshape(-1, span), band_matrix(fir_taps, frames, span),...  41.9 us
    dot_general x1, matrix products, decimate(): jnp.dot(signal.reshape(-1, span), band_matrix(fir_taps, frames, 0), preci...  41.9 us
    all_gather x1, waiting for transfers between devices, body(): gathered = lax.all_gather(local_spectra, 'sta', axis=0, tiled=True)  31.2 us
    reduce_sum x1, other arithmetic, cross_spectra(): real_sum = jnp.sum(local_re * remote_re + local_im * remote_im, axis=4)  13 us
  transfers between devices with their start and end apart: 3, of which 3 were waited for; matrix products, arithmetic and copies ran while one was open for 0% of the time, Pallas kernels for 0%

commit v1 on v0

--- a/solution.py
+++ b/solution.py
@@ -1,8 +1,12 @@
+import functools
 import math
 
 import jax
 import jax.numpy as jnp
+import numpy as np
 from jax import lax
+from jax.experimental import pallas as pl
+from jax.experimental.pallas import tpu as pltpu
 from jax.sharding import PartitionSpec as P
 
 BINS = 2048
@@ -11,6 +15,393 @@
 TAPS = 64
 OFFS = 2
 LAGS = 1024
+ROWS = 24
+PADROWS = 32
+FRAMES = 128
+SPLIT = 32
+WINDOW = 640
+GROUPSLOTS = 32
+TILES = 8
+MESH = pl.DeviceIdType.MESH
+VMEM_LIMIT = 56 * 1024 * 1024
+HIGHEST = lax.Precision.HIGHEST
+
+
+def constant_tables():
+    i = np.arange(128)
+    k = np.arange(32)[:, None]
+    turn = 2.0 * np.pi / 4096
+    twiddle = np.concatenate([np.cos(turn * k * i), -np.sin(turn * k * i)], 0).astype(np.float32)
+    q = np.arange(64)
+    fine = 2.0 * np.pi / 128 * (i[:, None] * q[None, :] % 128)
+    second = np.concatenate([np.cos(fine), np.sin(fine)], 0).astype(np.float32)
+    lag = np.arange(1024) - 512
+    slow = turn * (k * lag[None, :] % 4096)
+    lag_slow = np.concatenate([np.cos(slow), np.sin(slow)], 0).astype(np.float32)
+    quick = np.zeros((128, 256))
+    angle = 2.0 * np.pi / 128 * (q[:, None] * i[None, :] % 128)
+    quick[:64, :128] = np.cos(angle)
+    quick[:64, 128:] = np.sin(angle)
+    return twiddle, second, lag_slow, quick.astype(np.float32)
+
+
+def real_fft(values):
+    n = len(values)
+    if n == 2:
+        return [(values[0] + values[1], None), (values[0] - values[1], None)]
+    even = real_fft(values[0::2])
+    odd = real_fft(values[1::2])
+    result = [None] * (n // 2 + 1)
+    for k in range(n // 4 + 1):
+        er, ei = even[k]
+        orr, oi = odd[k]
+        c, s = math.cos(2 * math.pi * k / n), math.sin(2 * math.pi * k / n)
+        if k == 0:
+            tr, ti = orr, oi
+        elif 4 * k == n:
+            tr, ti = oi, -orr
+        elif oi is None:
+            tr, ti = orr * c, orr * (-s)
+        else:
+            tr, ti = orr * c + oi * s, oi * c - orr * s
+        def plus(a, b):
+            return b if a is None else a if b is None else a + b
+        def minus(a, b):
+            return (None if b is None else -b) if a is None else a if b is None else a - b
+        result[k] = (plus(er, tr), plus(ei, ti))
+        if n // 2 - k != k:
+            low = minus(ti, ei)
+            result[n // 2 - k] = (minus(er, tr), low)
+    return result
+
+
+def spectra_kernel(bands, live, taps, x_ref, tw_ref, second_ref, out_ref, band_scr, lhs1, dec, lhs2, wide, w2):
+    f32, bf16 = jnp.float32, jnp.bfloat16
+    a_index = lax.broadcasted_iota(jnp.int32, (WINDOW // 4, FRAMES), 0)
+    o_index = lax.broadcasted_iota(jnp.int32, (WINDOW // 4, FRAMES), 1)
+    lead = o_index - a_index + 32
+    pieces = [jnp.zeros((WINDOW // 4, FRAMES), f32)] * 4
+    for d in range(17):
+        here = lead == d
+        for b in range(4):
+            if 0 <= 4 * d - b < 64:
+                pieces[b] = jnp.where(here, taps[4 * d - b], pieces[b])
+    for b in range(4):
+        band_scr[pl.ds(b, WINDOW // 4, stride=4), :] = pieces[b]
+    band = band_scr[...]
+    high = band.astype(bf16)
+    low = (band - high.astype(f32)).astype(bf16)
+    weights = jnp.concatenate([high, low], axis=1)
+
+    for j in range(SPLIT):
+        rows = pl.ds(PADROWS * j, PADROWS)
+        if j == 0:
+            lhs1[rows, 0:128] = jnp.zeros((PADROWS, 128), bf16)
+            lhs1[rows, 128:] = x_ref[:, 0:512]
+        else:
+            lhs1[rows, :] = x_ref[:, 512 * j - 128:512 * j + 512]
+    summed = jnp.dot(lhs1[...], weights, preferred_element_type=f32)
+    dec[...] = (summed[:, :128] + summed[:, 128:]).astype(bf16).astype(f32)
+
+    q = lax.broadcasted_iota(jnp.int32, (64, 128), 0)
+    lane = lax.broadcasted_iota(jnp.int32, (64, 128), 1)
+    used = jnp.zeros((64, 128), jnp.bool_)
+    for b in range(4):
+        used = used | ((bands[0, b] < 32 * q + 32) & (bands[1, b] > 32 * q))
+    usedf = jnp.where(used, 1.0, 0.0).astype(f32)
+    q64 = lax.broadcasted_iota(jnp.int32, (64, 64), 0)
+    p64 = lax.broadcasted_iota(jnp.int32, (64, 64), 1)
+    before = jnp.where(p64 < q64, 1.0, 0.0).astype(f32)
+    rank = jnp.dot(before, usedf, preferred_element_type=f32)
+    pick = used & (rank == (lane % GROUPSLOTS).astype(f32))
+    pickf = jnp.where(pick, 1.0, 0.0).astype(f32)
+    group = jnp.sum(pickf * q.astype(f32), axis=0, keepdims=True)
+    chosen = jnp.dot(second_ref[...].astype(bf16), pickf.astype(bf16), preferred_element_type=f32)
+    cos_all, sin_all = chosen[:128], chosen[128:]
+    lane128 = lax.broadcasted_iota(jnp.int32, (128, 128), 1)
+    for kk in range(4):
+        mine = lane128 // GROUPSLOTS == kk
+        c = jnp.where(mine, cos_all, 0.0).astype(bf16)
+        s = jnp.where(mine, sin_all, 0.0)
+        w2[pl.ds(256 * kk, 128), 0:128] = c
+        w2[pl.ds(256 * kk, 128), 128:256] = (-s).astype(bf16)
+        w2[pl.ds(256 * kk + 128, 128), 0:128] = s.astype(bf16)
+        w2[pl.ds(256 * kk + 128, 128), 128:256] = c
+
+    def transform(chunk, carry):
+        values = [dec[pl.ds(PADROWS * j + 8 * chunk, 8), :] for j in range(SPLIT)]
+        freq = real_fft(values)
+        for k1 in range(32):
+            ar, ai = freq[k1] if k1 <= 16 else freq[32 - k1]
+            c = tw_ref[pl.ds(k1, 1), :]
+            s = tw_ref[pl.ds(32 + k1, 1), :]
+            if ai is None:
+                br, bi = ar * c, ar * s
+            elif k1 <= 16:
+                br, bi = ar * c - ai * s, ar * s + ai * c
+            else:
+                br, bi = ar * c + ai * s, ar * s - ai * c
+            rows = pl.ds((k1 // 4) * ROWS + 8 * chunk, 8)
+            column = (k1 % 4) * 256
+            lhs2[rows, column:column + 128] = br
+            lhs2[rows, column + 128:column + 256] = bi
+        return carry
+
+    lax.fori_loop(0, 3, transform, 0)
+    y = jnp.dot(lhs2[...].astype(bf16), w2[...], preferred_element_type=f32)
+    re, im = y[:, :128], y[:, 128:]
+    power = re * re + im * im
+    slot = lax.broadcasted_iota(jnp.int32, (1, 128), 1)
+    bins = [4 * t + slot // GROUPSLOTS + 32 * group.astype(jnp.int32) for t in range(TILES)]
+    gains = [jnp.zeros((ROWS, 128), f32)] * TILES
+    station = lax.broadcasted_iota(jnp.int32, (ROWS, 1), 0)
+    alive = jnp.where(station < 12, live[0].astype(f32), live[1].astype(f32))
+    for b in range(4):
+        total = jnp.zeros((ROWS, 128), f32)
+        inside = []
+        for t in range(TILES):
+            m = (bins[t] >= bands[0, b]) & (bins[t] < bands[1, b])
+            inside.append(m)
+            total = total + jnp.where(m, power[ROWS * t:ROWS * t + ROWS], 0.0)
+        width = (bands[1, b] - bands[0, b]).astype(f32)
+        energy = jnp.sum(total, axis=1, keepdims=True) / width
+        scale = lax.rsqrt(energy + 1e-06) * alive
+        for t in range(TILES):
+            gains[t] = gains[t] + jnp.where(inside[t], scale, 0.0)
+    for t in range(TILES):
+        rows = slice(ROWS * t, ROWS * t + ROWS)
+        wre = re[rows] * gains[t]
+        wim = im[rows] * gains[t]
+        wide[pl.ds(t, ROWS, stride=16), :] = wre
+        wide[pl.ds(8 + t, ROWS, stride=16), :] = wim
+    out_ref[...] = wide[...].astype(bf16)
+
+
+def smem():
+    return pl.BlockSpec(memory_space=pltpu.SMEM)
+
+
+def vmem():
+    return pl.BlockSpec(memory_space=pltpu.VMEM)
+
+
+def local_spectra(records, fir_taps, edges, station_live):
+    twiddle, second, _, _ = constant_tables()
+    x = jnp.transpose(records, (0, 2, 1, 3)).reshape(ROWS, -1)
+    x = jnp.pad(x, ((0, PADROWS - ROWS), (0, 0)))
+    f32, bf16 = jnp.float32, jnp.bfloat16
+    return pl.pallas_call(
+        spectra_kernel,
+        out_shape=jax.ShapeDtypeStruct((ROWS * 16, 128), bf16),
+        in_specs=[smem(), smem(), smem(), vmem(), vmem(), vmem()],
+        out_specs=vmem(),
+        scratch_shapes=[
+            pltpu.VMEM((WINDOW, FRAMES), f32),
+            pltpu.VMEM((PADROWS * SPLIT, WINDOW), bf16),
+            pltpu.VMEM((PADROWS * SPLIT, FRAMES), f32),
+            pltpu.VMEM((ROWS * TILES, 1024), f32),
+            pltpu.VMEM((ROWS * 16, 128), f32),
+            pltpu.VMEM((1024, 256), bf16),
+        ],
+        compiler_params=pltpu.CompilerParams(vmem_limit_bytes=VMEM_LIMIT),
+        name="spectra",
+    )(edges, station_live, fir_taps, x, twiddle, second)
+
+
+def correlate_kernel(bands, kept, local_ref, remote_ref, slow_ref, quick_ref, out_ref, left, cross, lhs, table):
+    f32, bf16 = jnp.float32, jnp.bfloat16
+    left[...] = local_ref[...].astype(f32)
+
+    def pairs(block, carry):
+        k = block // 8
+        s = block % 8
+        for i2 in range(2):
+            for b in range(3):
+                rre, rim = [], []
+                for w in range(4):
+                    r = remote_ref[block, pl.ds((i2 * 12 + b * 4 + w) * 16, 16), :].astype(f32)
+                    rre.append(r[0:8])
+                    rim.append(r[8:16])
+                for ia in range(6):
+                    re = im = None
+                    for w in range(4):
+                        base = (ia * 4 + w) * 16
+                        lre = left[base:base + 8, :]
+                        lim = left[base + 8:base + 16, :]
+                        pre = lre * rre[w] + lim * rim[w]
+                        pim = lim * rre[w] - lre * rim[w]
+                        re = pre if re is None else re + pre
+                        im = pim if im is None else im + pim
+                    row = k * 288 + ia * 48 + s * 6 + i2 * 3 + b
+                    cross[pl.ds(row, 8, stride=1152), :] = re
+                    cross[pl.ds(row + 576, 8, stride=1152), :] = im
+        return carry
+
+    lax.fori_loop(0, 16, pairs, 0)
+
+    q = lax.broadcasted_iota(jnp.int32, (GROUPSLOTS, 128), 1)
+    used = jnp.zeros((GROUPSLOTS, 128), jnp.bool_)
+    for b in range(4):
+        used = used | ((bands[0, b] < 32 * q + 32) & (bands[1, b] > 32 * q))
+    used = used & (q < 64)
+    usedf = jnp.where(used, 1.0, 0.0).astype(f32)
+    p0 = lax.broadcasted_iota(jnp.int32, (128, 128), 0)
+    p1 = lax.broadcasted_iota(jnp.int32, (128, 128), 1)
+    before = jnp.where(p0 < p1, 1.0, 0.0).astype(f32)
+    rank = jnp.dot(usedf, before, preferred_element_type=f32)
+    g = lax.broadcasted_iota(jnp.int32, (GROUPSLOTS, 128), 0)
+    pick = jnp.where(used & (rank == g.astype(f32)), 1.0, 0.0).astype(f32)
+    quick = jnp.dot(pick, quick_ref[...], precision=HIGHEST, preferred_element_type=f32)
+    quick = quick * f32(1.0 / math.sqrt(2048))
+    qc, qs = quick[:, :128], quick[:, 128:]
+    zero_bin = jnp.where((pick[:, 0:1] > 0.5), 0.5, 1.0)
+
+    for t in range(TILES):
+        for h in range(2):
+            column = 256 * t + 128 * h
+            lhs[:, column:column + 128] = cross[pl.ds(1152 * t + 576 * h, 576), :].astype(bf16)
+        for kk in range(4):
+            k1 = 4 * t + kk
+            row = 256 * t + 32 * kk
+            for n in range(8):
+                lanes = slice(128 * n, 128 * n + 128)
+                sc = slow_ref[pl.ds(k1, 1), lanes]
+                ss = slow_ref[pl.ds(32 + k1, 1), lanes]
+                wc = sc * qc - ss * qs
+                ws = -(ss * qc + sc * qs)
+                if k1 == 0:
+                    wc, ws = wc * zero_bin, ws * zero_bin
+                table[pl.ds(row, 32), lanes] = wc.astype(bf16)
+                table[pl.ds(row + 128, 32), lanes] = ws.astype(bf16)
+    for n in range(4):
+        res = jnp.dot(lhs[...], table[:, 256 * n:256 * n + 256], preferred_element_type=f32)
+        for k in range(2):
+            part = res[288 * k:288 * k + 288] * kept[k].astype(f32)
+            for h in range(2):
+                out_ref[pl.ds((2 * n + h) * 2 + k, 288, stride=16), :] = part[:, 128 * h:128 * h + 128]
+
+
+def correlate(local, remote, edges, block_live):
+    _, _, slow, quick = constant_tables()
+    f32, bf16 = jnp.float32, jnp.bfloat16
+    out = pl.pallas_call(
+        correlate_kernel,
+        out_shape=jax.ShapeDtypeStruct((288 * 16, 128), f32),
+        in_specs=[smem(), smem(), vmem(), vmem(), vmem(), vmem()],
+        out_specs=vmem(),
+        scratch_shapes=[
+            pltpu.VMEM((ROWS * 16, 128), f32),
+            pltpu.VMEM((1152 * TILES, 128), f32),
+            pltpu.VMEM((576, 2048), bf16),
+            pltpu.VMEM((2048, 1024), bf16),
+        ],
+        compiler_params=pltpu.CompilerParams(vmem_limit_bytes=VMEM_LIMIT),
+        name="correlate",
+    )(edges, block_live, local, remote, slow, quick)
+    out = out.reshape(288, 8, 2, 128)
+    return jnp.transpose(out, (0, 2, 1, 3)).reshape(288, 2, 1024)
+
+
+def gather_kernel(parts, own_ref, out_ref, own_send, x_send, core_send, recv):
+    section, grp, sta = lax.axis_index("section"), lax.axis_index("grp"), lax.axis_index("sta")
+    groups = 16
+    r = section * groups + grp
+    mate = sta + 1 - 2 * lax.rem(sta, 2)
+    peers = [lax.rem(sta + 2 * d, 8) for d in (1, 2, 3)]
+
+    def at(shift):
+        g = lax.rem(r + shift + 32, 32)
+        return (g // groups, lax.rem(g, groups), sta)
+
+    def near(s):
+        return (section, grp, s)
+
+    barrier = pltpu.get_barrier_semaphore()
+    partners = [at(1), at(2), at(-1), at(-2), near(mate)] + [near(p) for p in peers]
+    for who in partners:
+        pl.semaphore_signal(barrier, inc=1, device_id=who, device_id_type=MESH)
+    pl.semaphore_wait(barrier, len(partners))
+
+    rows = own_ref.shape[0] // parts
+    started = []
+
+    def send(src, k, s, c, sem, who):
+        copy = pltpu.make_async_remote_copy(
+            src_ref=src,
+            dst_ref=out_ref.at[k * 8 + s, pl.ds(c * rows, rows), :],
+            send_sem=sem,
+            recv_sem=recv.at[k * 8 + s, c],
+            device_id=who,
+            device_id_type=MESH,
+        )
+        copy.start()
+        started.append(copy)
+
+    def held(k, s, c):
+        return out_ref.at[k * 8 + s, pl.ds(c * rows, rows), :]
+
+    def arrived(k, s, c):
+        pltpu.make_async_remote_copy(
+            src_ref=held(k, s, c),
+            dst_ref=held(k, s, c),
+            send_sem=own_send.at[0, 0],
+            recv_sem=recv.at[k * 8 + s, c],
+            device_id=near(mate),
+            device_id_type=MESH,
+        ).wait_recv()
+
+    for c in range(parts):
+        for k in range(2):
+            send(own_ref.at[pl.ds(c * rows, rows), :], k, sta, c, own_send.at[k, c], at(k + 1))
+    for c in range(parts):
+        for k in range(2):
+            arrived(k, sta, c)
+            for n, p in enumerate(peers):
+                send(held(k, sta, c), k, sta, c, x_send.at[k, n, c], near(p))
+            send(held(k, sta, c), k, sta, c, core_send.at[k, 0, c], near(mate))
+    for c in range(parts):
+        for k in range(2):
+            for n, p in enumerate(peers):
+                arrived(k, p, c)
+                send(held(k, p, c), k, p, c, core_send.at[k, n + 1, c], near(mate))
+    for c in range(parts):
+        for k in range(2):
+            for s in [mate] + [lax.rem(mate + 2 * d, 8) for d in (1, 2, 3)]:
+                arrived(k, s, c)
+    for copy in started:
+        copy.wait_send()
+
+
+def gather(local):
+    parts = 2
+    return pl.pallas_call(
+        functools.partial(gather_kernel, parts),
+        out_shape=jax.ShapeDtypeStruct((16,) + local.shape, local.dtype),
+        in_specs=[vmem()],
+        out_specs=vmem(),
+        scratch_shapes=[
+            pltpu.SemaphoreType.DMA((2, parts)),
+            pltpu.SemaphoreType.DMA((2, 3, parts)),
+            pltpu.SemaphoreType.DMA((2, 4, parts)),
+            pltpu.SemaphoreType.DMA((16, parts)),
+        ],
+        compiler_params=pltpu.CompilerParams(collective_id=0, has_side_effects=True, vmem_limit_bytes=VMEM_LIMIT),
+        name="gather",
+    )(local)
+
+
+def used_bins(records, fir_taps, band_bins, station_live, block_live):
+    edges = jnp.transpose(band_bins)
+    local = local_spectra(records, fir_taps, edges, station_live)
+    return correlate(local, gather(local), edges, block_live)
+
+
+def body(records, fir_taps, band_bins, station_live, block_live):
+    q = jnp.arange(64, dtype=jnp.int32)[:, None]
+    hit = (band_bins[None, :, 0] < 32 * q + 32) & (band_bins[None, :, 1] > 32 * q)
+    count = jnp.sum(jnp.any(hit, axis=1).astype(jnp.int32))
+    arguments = (records, fir_taps, band_bins, station_live, block_live)
+    return lax.cond(count <= GROUPSLOTS, used_bins, every_bin, *arguments)
 
 
 epsilon = 1e-06
@@ -133,7 +524,7 @@
     return result.reshape(row_count, block_count, LAGS) * kept_blocks[None, :, None]
 
 
-def body(records, fir_taps, band_bins, station_live, block_live):
+def every_bin(records, fir_taps, band_bins, station_live, block_live):
     decimated = decimate(records, fir_taps)
     real_part, imag_part = spectrum(decimated.reshape(-1, NT))
     out_shape = decimated.shape[:-1] + (BINS,)

time: 523 us -> 61.7 us (0.12)
  matrix products: 187 us -> 0 us
  other arithmetic: 160 us -> 0.73 us
  waiting for transfers between devices: 108 us -> 0 us
  local copies, waits for them, and re-layouts: 50.9 us -> 4.78 us
  Pallas kernels: 0 us -> 41.7 us
    dot_general x16 -> x0, matrix products: 187 us -> none  [the longest x4 97.4 us: inverse_advance(): jnp.dot(flattened, lag_table(frequency, parity, starts, block_width), pre...]
    another operation x10 -> x0, other arithmetic: 141 us -> none
    ppermute x2 -> x0, waiting for transfers between devices: 76.7 us -> none  [passed_along(): return lax.ppermute(block, axis, route)]
    pallas_call x0 -> x3, Pallas kernels: none -> 41.7 us  [the longest x1 28 us: gather(): pl.pallas_call(functools.partial(gather_kernel, parts), out_shape=jax.Sha...]
    all_gather x1 -> x0, waiting for transfers between devices: 31.2 us -> none  [body(): gathered = lax.all_gather(local_spectra, 'sta', axis=0, tiled=True)]
    another operation x6 -> x0, local copies, waits for them, and re-layouts: 18.5 us -> none  [the longest x1 9.47 us: body(): arrived = jnp.stack(pieces, axis=1)]
    reduce_sum x1, other arithmetic: 13 us -> 0.63 us  [body(): count = jnp.sum(jnp.any(hit, axis=1).astype(jnp.int32))]
    reshape x6 -> x1, local copies, waits for them, and re-layouts: 11.8 us -> 1.57 us  [local_spectra(): x = jnp.transpose(records, (0, 2, 1, 3)).reshape(ROWS, -1)]
  transfers between devices with their start and end apart: 3 -> 0, of which waited for: 3 -> 0; matrix products, arithmetic and copies ran while one was open for 0% -> 0% of each run, Pallas kernels for 0% -> 0%
where the time goes in v1:
time: 61.7 us; the launch traced here: 61.5 us
  Pallas kernels  41.7 us (68%)
  between operations  14 us (23%)
  local copies, waits for them, and re-layouts  4.78 us (8%)
  other arithmetic  0.73 us (1%)
    pallas_call x1, Pallas kernels, gather(): pl.pallas_call(functools.partial(gather_kernel, parts), out_shape=jax.Sha...  28 us
    pallas_call x1, Pallas kernels, correlate(): pl.pallas_call(correlate_kernel, out_shape=jax.ShapeDtypeStruct((288 * 16...  10 us
    pallas_call x1, Pallas kernels, local_spectra(): pl.pallas_call(spectra_kernel, out_shape=jax.ShapeDtypeStruct((ROWS * 16,...  3.59 us
    reshape x1, local copies, waits for them, and re-layouts, local_spectra(): x = jnp.transpose(records, (0, 2, 1, 3)).reshape(ROWS, -1)  1.57 us
    unnamed x2, local copies, waits for them, and re-layouts  1.4 us

profile of v1, /device:TPU:1, one launch (start us, length us, event | category | flops | bytes accessed | tf_op | source)
XLA Modules:
  0.0 61.5 jit_solution(17166714715893734899)
XLA Ops:
  6.5 0.8 %slice_bitcast_fusion.3 = (s32[4]{0:T(128)S(1)}, s32[4]{0:T(128)S(1)}) fusion(s32[4,2]{0,1:T(2,128)} %param.17), kind=kLoop, calls=%fused_computation.840 | loop fusion | bytes 64 | tf_op jit(solution)/shard_map/lt | solution.py:401
  7.3 0.1 and_reduce_fusion
  7.4 0.6 %convert_reduce_fusion = s32[]{:T(128)} fusion(pred[64]{0:T(512)(128)(4,1)S(1)} %and_reduce_fusion), kind=kLoop, calls=%fused_computation.837 | loop fusion | flops 127 | bytes 68 | tf_op jit(solution)/shard_map/reduce_sum | solution.py:402
  8.7 44.6 %conditional.1 = (f32[288,2,1024]{2,1,0:T(2,128)S(1)}) conditional(s32[]{:T(128)} %convert_element_type.114, (f32[64]{0:T(128)}, bf16[2,4,3,16384]{3,1,2,0:T(4,128)(2,1)}, s32[4,2]{0,1:T(2,128)}, s32[2]{0:T(128)}, s32[2]{0:T(128)}) %tuple.55, (s32[4,2]{0,1:T(2,128)}, bf16[2,4,3,16384]{3,1,2,0:T(4,128)(2,1)}, s32[2]{0:T(128)}, f32[64]{0:T(128)}, (), ...), branch_computations={%region_2.11_spmd, %region_11.12_spmd} | conditional | flops 2641577216 | bytes 128721696 | solution.py:404
  8.9 0.0 copy-start.2
  8.9 0.0 copy-start.5
  8.9 1.6 %reshape.261 = bf16[24,16384]{1,0:T(8,128)(2,1)S(1)} reshape(bf16[2,3,4,16384]{3,2,1,0:T(4,128)(2,1)} %bitcast.772) | data formatting | bytes 1572864 | tf_op jit(solution)/shard_map/cond/branch_1_fun/reshape | solution.py:190
  10.5 1.0 %pad.8.x_ref = bf16[32,16384]{1,0:T(8,128)(2,1)} pad(bf16[24,16384]{1,0:T(8,128)(2,1)S(1)} %reshape.261, bf16[]{:T(256)} %constant.246.clone), padding=0_8x0_0 | pad | bytes 1835010 | tf_op jit(solution)/shard_map/cond/branch_1_fun/jit(_pad)/pad | solution.py:191
  11.6 3.6 %spectra.1.own_ref.local_ref = bf16[384,128]{1,0:T(8,128)(2,1)} custom-call(s32[2,4]{1,0:T(2,128)} %bitcast.778, s32[2]{0:T(128)} %get-tuple-element.292.live, f32[64]{0:T(128)} %get-tuple-element.293.taps, bf16[32,16384]{1,0:T(8,128)(2,1)} %pad.8.x_ref, f32[64,128]{1,0:T(8,128)} %constant.250.clone.1.tw_ref, f32[256,64]{1,0:T(8,128)} %constant.251.clone.1.second_ref), custom_call_target="tpu_custom_call" | custom-call | tf_op jit(solution)/shard_map/cond/branch_1_fun/spectra/pallas_call | solution.py:193
  15.1 28.0 %gather.9.remote_ref = bf16[16,384,128]{2,1,0:T(8,128)(2,1)} custom-call(bf16[384,128]{1,0:T(8,128)(2,1)} %spectra.1.own_ref.local_ref), custom_call_target="tpu_custom_call" | custom-call | tf_op jit(solution)/shard_map/cond/branch_1_fun/gather/pallas_call | solution.py:377
  43.2 0.0 copy-done.2
  43.2 0.0 copy-done.5
  43.2 10.0 %correlate.1 = f32[4608,128]{1,0:T(8,128)S(1)} custom-call(s32[2,4]{1,0:T(2,128)S(1)} %bitcast.779, s32[2]{0:T(128)S(1)} %copy-done.5, bf16[384,128]{1,0:T(8,128)(2,1)} %spectra.1.own_ref.local_ref, bf16[16,384,128]{2,1,0:T(8,128)(2,1)} %gather.9.remote_ref, f32[64,1024]{1,0:T(8,128)} %constant.252.clone.1.slow_ref, f32[128,256]{1,0:T(8,128)} %constant.253.clone.1.quick_ref), custom_call_target="tpu_custom_call" | custom-call | tf_op jit(solution)/shard_map/cond/branch_1_fun/correlate/pallas_call | solution.py:287
  53.2 0.0 copy-start
  53.3 1.4 %copy-done = f32[288,2,1024]{2,1,0:T(2,128)} copy-done((f32[288,2,1024]{2,1,0:T(2,128)}, f32[288,2,1024]{2,1,0:T(2,128)S(1)}, u32[]{:S(2)}) %copy-start) | copy-done | bytes 2359320
  (1 shorter events, 0.0 us)
Async XLA Ops:
  8.9 34.3 %copy-start.2 = (s32[4,2]{0,1:T(2,128)S(1)}, s32[4,2]{0,1:T(2,128)}, u32[]{:S(2)}) copy-start(s32[4,2]{0,1:T(2,128)} %get-tuple-element.290) | copy-start | bytes 100 | tf_op jit(solution)/shard_map/cond
  8.9 34.3 %copy-start.5 = (s32[2]{0:T(128)S(1)}, s32[2]{0:T(128)}, u32[]{:S(2)}) copy-start(s32[2]{0:T(128)} %get-tuple-element.291.kept) | copy-start | bytes 28 | tf_op jit(solution)/shard_map/cond
  53.2 1.4 %copy-start = (f32[288,2,1024]{2,1,0:T(2,128)}, f32[288,2,1024]{2,1,0:T(2,128)S(1)}, u32[]{:S(2)}) copy-start(f32[288,2,1024]{2,1,0:T(2,128)S(1)} %get-tuple-element.565) | copy-start | bytes 7077892

commit v2 on v0

v2 whole, which is shorter than its diff:
```python
import functools
import math

import jax
import jax.numpy as jnp
import numpy as np
from jax import lax
from jax.experimental import pallas as pl
from jax.experimental.pallas import tpu as pltpu
from jax.sharding import PartitionSpec as P

ROWS = 24
PADROWS = 32
FRAMES = 128
SPLIT = 32
WINDOW = 640
TILES = 8
MESH = pl.DeviceIdType.MESH
VMEM_LIMIT = 40 * 1024 * 1024
HIGHEST = lax.Precision.HIGHEST


def constant_tables():
    i = np.arange(128)
    k = np.arange(32)[:, None]
    turn = 2.0 * np.pi / 4096
    twiddle = np.concatenate([np.cos(turn * k * i), -np.sin(turn * k * i)], 0).astype(np.float32)
    q = np.arange(64)
    fine = 2.0 * np.pi / 128 * (i[:, None] * q[None, :] % 128)
    second = np.concatenate([np.cos(fine), np.sin(fine)], 0).astype(np.float32)
    lag = np.arange(1024) - 512
    slow = turn * (k * lag[None, :] % 4096)
    lag_slow = np.concatenate([np.cos(slow), np.sin(slow)], 0).astype(np.float32)
    quick = np.zeros((128, 256))
    angle = 2.0 * np.pi / 128 * (q[:, None] * i[None, :] % 128)
    quick[:64, :128] = np.cos(angle)
    quick[:64, 128:] = np.sin(angle)
    return twiddle, second, lag_slow, quick.astype(np.float32)


def real_fft(values):
    n = len(values)
    if n == 2:
        return [(values[0] + values[1], None), (values[0] - values[1], None)]
    even = real_fft(values[0::2])
    odd = real_fft(values[1::2])
    result = [None] * (n // 2 + 1)
    for k in range(n // 4 + 1):
        er, ei = even[k]
        orr, oi = odd[k]
        c, s = math.cos(2 * math.pi * k / n), math.sin(2 * math.pi * k / n)
        if k == 0:
            tr, ti = orr, oi
        elif 4 * k == n:
            tr, ti = oi, -orr
        elif oi is None:
            tr, ti = orr * c, orr * (-s)
        else:
            tr, ti = orr * c + oi * s, oi * c - orr * s
        def plus(a, b):
            return b if a is None else a if b is None else a + b
        def minus(a, b):
            return (None if b is None else -b) if a is None else a if b is None else a - b
        result[k] = (plus(er, tr), plus(ei, ti))
        if n // 2 - k != k:
            low = minus(ti, ei)
            result[n // 2 - k] = (minus(er, tr), low)
    return result


def filter_weights(taps, band_scr):
    f32, bf16 = jnp.float32, jnp.bfloat16
    a_index = lax.broadcasted_iota(jnp.int32, (WINDOW // 4, FRAMES), 0)
    o_index = lax.broadcasted_iota(jnp.int32, (WINDOW // 4, FRAMES), 1)
    lead = o_index - a_index + 32
    pieces = [jnp.zeros((WINDOW // 4, FRAMES), f32)] * 4
    for d in range(17):
        here = lead == d
        for b in range(4):
            if 0 <= 4 * d - b < 64:
                pieces[b] = jnp.where(here, taps[4 * d - b], pieces[b])
    for b in range(4):
        band_scr[pl.ds(b, WINDOW // 4, stride=4), :] = pieces[b]
    band = band_scr[...]
    high = band.astype(bf16)
    low = (band - high.astype(f32)).astype(bf16)
    return jnp.concatenate([high, low], axis=1)


def by_band(index, values):
    result = jnp.full(index.shape, values[3], jnp.int32)
    for b in range(3):
        result = jnp.where(index == b, values[b], result)
    return result


def band_edges(bands):
    first = [bands[0, b] for b in range(4)]
    last = [bands[1, b] for b in range(4)]
    return first, last, [s // 32 for s in first], [s % 32 for s in first]


def second_stage(bands, second_ref, w2):
    f32, bf16 = jnp.float32, jnp.bfloat16
    _, _, coarse, _ = band_edges(bands)
    q = lax.broadcasted_iota(jnp.int32, (64, 128), 0)
    lane = lax.broadcasted_iota(jnp.int32, (64, 128), 1)
    base = by_band(lane % 32 // 8, coarse) + lane % 8
    lane128 = lax.broadcasted_iota(jnp.int32, (128, 128), 1)
    for late in range(2):
        pick = jnp.where(q == base + late, 1.0, 0.0).astype(bf16)
        chosen = jnp.dot(second_ref[...].astype(bf16), pick, preferred_element_type=f32)
        for kk in range(4):
            mine = lane128 // 32 == kk
            c = jnp.where(mine, chosen[:128], 0.0)
            s = jnp.where(mine, chosen[128:], 0.0)
            top, under = pl.ds(256 * kk, 128), pl.ds(256 * kk + 128, 128)
            re, im = slice(256 * late, 256 * late + 128), slice(256 * late + 128, 256 * late + 256)
            w2[top, re] = c.astype(bf16)
            w2[top, im] = (-s).astype(bf16)
            w2[under, re] = s.astype(bf16)
            w2[under, im] = c.astype(bf16)


def transform(dec, tw_ref, lhs2):
    def one(chunk, carry):
        values = [dec[pl.ds(PADROWS * j + 8 * chunk, 8), :] for j in range(SPLIT)]
        freq = real_fft(values)
        for k1 in range(32):
            ar, ai = freq[k1] if k1 <= 16 else freq[32 - k1]
            c = tw_ref[pl.ds(k1, 1), :]
            s = tw_ref[pl.ds(32 + k1, 1), :]
            if ai is None:
                br, bi = ar * c, ar * s
            elif k1 <= 16:
                br, bi = ar * c - ai * s, ar * s + ai * c
            else:
                br, bi = ar * c + ai * s, ar * s - ai * c
            rows = pl.ds((k1 // 4) * ROWS + 8 * chunk, 8)
            column = (k1 % 4) * 256
            lhs2[rows, column:column + 128] = br
            lhs2[rows, column + 128:column + 256] = bi
        return carry

    lax.fori_loop(0, 3, one, 0)


def whiten_slots(bands, live, y, wide):
    f32 = jnp.float32
    first, last, coarse, fine = band_edges(bands)
    slot = lax.broadcasted_iota(jnp.int32, (1, 128), 1)
    owner = slot % 32 // 8
    base = by_band(owner, coarse) + slot % 8
    offset = by_band(owner, fine)
    re, im, inside, counted = [], [], [], []
    for t in range(TILES):
        k1 = 4 * t + slot // 32
        late = k1 < offset
        bins = k1 + 32 * (base + jnp.where(late, 1, 0))
        rows = slice(ROWS * t, ROWS * t + ROWS)
        re.append(jnp.where(late, y[rows, 256:384], y[rows, 0:128]))
        im.append(jnp.where(late, y[rows, 384:512], y[rows, 128:256]))
        within = [(bins >= first[b]) & (bins < last[b]) for b in range(4)]
        inside.append(within)
        own = within[0] & (owner == 0)
        for b in range(1, 4):
            mine = within[b] & (owner == b)
            for earlier in range(b):
                mine = mine & jnp.logical_not(within[earlier])
            own = own | mine
        counted.append(own)
    station = lax.broadcasted_iota(jnp.int32, (ROWS, 1), 0)
    alive = jnp.where(station < 12, live[0].astype(f32), live[1].astype(f32))
    gains = [jnp.zeros((ROWS, 128), f32)] * TILES
    for b in range(4):
        total = jnp.zeros((ROWS, 128), f32)
        for t in range(TILES):
            power = re[t] * re[t] + im[t] * im[t]
            total = total + jnp.where(inside[t][b] & (owner == b), power, 0.0)
        width = (last[b] - first[b]).astype(f32)
        energy = jnp.sum(total, axis=1, keepdims=True) / width
        scale = lax.rsqrt(energy + 1e-06) * alive
        for t in range(TILES):
            gains[t] = gains[t] + jnp.where(inside[t][b], scale, 0.0)
    for t in range(TILES):
        gain = jnp.where(counted[t], gains[t], 0.0)
        wide[pl.ds(t, ROWS, stride=16), :] = re[t] * gain
        wide[pl.ds(8 + t, ROWS, stride=16), :] = im[t] * gain


def lag_groups(bands, quick_ref):
    f32 = jnp.float32
    _, _, coarse, fine = band_edges(bands)
    g = lax.broadcasted_iota(jnp.int32, (32, 128), 0)
    q = lax.broadcasted_iota(jnp.int32, (32, 128), 1)
    base = by_band(g // 8, coarse) + g % 8
    offset = by_band(g // 8, fine)
    tables = []
    for late in range(2):
        pick = jnp.where(q == base + late, 1.0, 0.0).astype(f32)
        quick = jnp.dot(pick, quick_ref[...], precision=HIGHEST, preferred_element_type=f32)
        quick = quick * f32(1.0 / math.sqrt(2048))
        tables.append((quick[:, :128], quick[:, 128:]))
    return base, offset, tables


def lag_tile(t, base, offset, tables, slow_ref, table):
    bf16 = jnp.bfloat16
    for kk in range(4):
        k1 = 4 * t + kk
        late = k1 < offset
        qc = jnp.where(late, tables[1][0], tables[0][0])
        qs = jnp.where(late, tables[1][1], tables[0][1])
        if k1 == 0:
            half = jnp.where(base + jnp.where(late, 1, 0) == 0, 0.5, 1.0)
            qc, qs = qc * half, qs * half
        row = 256 * t + 32 * kk
        for n in range(8):
            lanes = slice(128 * n, 128 * n + 128)
            sc = slow_ref[pl.ds(k1, 1), lanes]
            ss = slow_ref[pl.ds(32 + k1, 1), lanes]
            table[pl.ds(row, 32), lanes] = (sc * qc - ss * qs).astype(bf16)
            table[pl.ds(row + 128, 32), lanes] = (-(ss * qc + sc * qs)).astype(bf16)


def cross_block(left, got, cross, k, s):
    f32 = jnp.float32
    for i2 in range(2):
        for b in range(3):
            rre, rim = [], []
            for w in range(4):
                r = got[k * 8 + s, pl.ds((i2 * 12 + b * 4 + w) * 16, 16), :].astype(f32)
                rre.append(r[0:8])
                rim.append(r[8:16])
            for ia in range(6):
                re = im = None
                for w in range(4):
                    at = (ia * 4 + w) * 16
                    lre = left[at:at + 8, :]
                    lim = left[at + 8:at + 16, :]
                    pre = lre * rre[w] + lim * rim[w]
                    pim = lim * rre[w] - lre * rim[w]
                    re = pre if re is None else re + pre
                    im = pim if im is None else im + pim
                row = k * 288 + ia * 48 + s * 6 + i2 * 3 + b
                cross[pl.ds(row, 8, stride=1152), :] = re
                cross[pl.ds(row + 576, 8, stride=1152), :] = im


def whole_kernel(parts, bands, live, taps, kept, x_any, tw_ref, second_ref, slow_ref, quick_ref, out_ref,
                 x_in, band_scr, lhs1, dec, lhs2, wide, w2, own_ref, got, cross, lhs, table,
                 x_sem, y_send, x_send, f_send, m_send, recv):
    f32, bf16 = jnp.float32, jnp.bfloat16
    section, grp, sta = lax.axis_index("section"), lax.axis_index("grp"), lax.axis_index("sta")
    groups = 16
    r = section * groups + grp
    mate = sta + 1 - 2 * lax.rem(sta, 2)
    right, across, left_peer = [lax.rem(sta + 2 * d, 8) for d in (1, 2, 3)]

    def group_at(shift):
        g = lax.rem(r + shift + 32, 32)
        return (g // groups, lax.rem(g, groups), sta)

    def near(s):
        return (section, grp, s)

    barrier = pltpu.get_barrier_semaphore()
    partners = [group_at(1), group_at(-1), near(mate), near(right), near(left_peer)]
    for who in partners:
        pl.semaphore_signal(barrier, inc=1, device_id=who, device_id_type=MESH)

    fetches = [pltpu.make_async_copy(x_any.at[n], x_in.at[n], x_sem.at[n]) for n in range(6)]
    for fetch in fetches:
        fetch.start()
    weights = filter_weights(taps, band_scr)
    second_stage(bands, second_ref, w2)
    for fetch in fetches:
        fetch.wait()
    x = x_in[...].reshape(ROWS, -1)
    x = jnp.concatenate([x, jnp.zeros((PADROWS - ROWS, x.shape[1]), bf16)], axis=0)
    for j in range(SPLIT):
        rows = pl.ds(PADROWS * j, PADROWS)
        if j == 0:
            lhs1[rows, 0:128] = jnp.zeros((PADROWS, 128), bf16)
            lhs1[rows, 128:] = x[:, 0:512]
        else:
            lhs1[rows, :] = x[:, 512 * j - 128:512 * j + 512]
    summed = jnp.dot(lhs1[...], weights, preferred_element_type=f32)
    dec[...] = (summed[:, :128] + summed[:, 128:]).astype(bf16).astype(f32)
    transform(dec, tw_ref, lhs2)
    y = jnp.dot(lhs2[...].astype(bf16), w2[...], preferred_element_type=f32)
    whiten_slots(bands, live, y, wide)
    own_ref[...] = wide[...].astype(bf16)

    pl.semaphore_wait(barrier, len(partners))
    rows = own_ref.shape[0] // parts
    started = []

    def held(k, s, c):
        return got.at[k * 8 + s, pl.ds(c * rows, rows), :]

    def send(src, k, s, c, sem, who):
        copy = pltpu.make_async_remote_copy(
            src_ref=src, dst_ref=held(k, s, c), send_sem=sem, recv_sem=recv.at[k * 8 + s, c],
            device_id=who, device_id_type=MESH,
        )
        copy.start()
        started.append(copy)

    def arrived(k, s, c):
        pltpu.make_async_remote_copy(
            src_ref=held(k, s, c), dst_ref=held(k, s, c), send_sem=y_send.at[0, 0],
            recv_sem=recv.at[k * 8 + s, c], device_id=near(mate), device_id_type=MESH,
        ).wait_recv()

    def own_column(k, c):
        arrived(k, sta, c)
        if k == 0:
            send(held(0, sta, c), 1, sta, c, y_send.at[1, c], group_at(1))
        send(held(k, sta, c), k, sta, c, x_send.at[k, 0, c], near(right))
        send(held(k, sta, c), k, sta, c, x_send.at[k, 1, c], near(left_peer))
        send(held(k, sta, c), k, sta, c, m_send.at[k, 0, c], near(mate))

    def from_left(k, c):
        arrived(k, left_peer, c)
        if 2 * c < parts:
            send(held(k, left_peer, c), k, left_peer, c, f_send.at[k, c], near(right))
        send(held(k, left_peer, c), k, left_peer, c, m_send.at[k, 1, c], near(mate))

    def from_right(k, c):
        arrived(k, right, c)
        if 2 * c >= parts:
            send(held(k, right, c), k, right, c, f_send.at[k, c], near(left_peer))
        send(held(k, right, c), k, right, c, m_send.at[k, 2, c], near(mate))

    def from_across(k, c):
        arrived(k, across, c)
        send(held(k, across, c), k, across, c, m_send.at[k, 3, c], near(mate))

    def sides(k):
        for c in range(parts):
            from_left(k, c)
            from_right(k, parts - 1 - c)

    def far(k):
        for c in range(parts // 2):
            from_across(k, c)
            from_across(k, parts // 2 + c)

    def by_mate(k, s):
        for c in range(parts):
            arrived(k, s, c)

    def several(k, start, count):
        def one(n, carry):
            cross_block(wide, got, cross, k, lax.rem(start + 2 * n, 8))
            return carry
        lax.fori_loop(0, count, one, 0)

    def pack(k):
        rows = pl.ds(288 * k, 288)
        for t in range(TILES):
            for h in range(2):
                column = 256 * t + 128 * h
                lhs[rows, column:column + 128] = cross[pl.ds(1152 * t + 576 * h + 288 * k, 288), :].astype(bf16)

    def product(k, n):
        part = jnp.dot(lhs[pl.ds(288 * k, 288), :], table[:, 256 * n:256 * n + 256], preferred_element_type=f32)
        part = part * kept[k].astype(f32)
        for h in range(2):
            out_ref[pl.ds((2 * n + h) * 2 + k, 288, stride=16), :] = part[:, 128 * h:128 * h + 128]

    for c in range(parts):
        send(own_ref.at[pl.ds(c * rows, rows), :], 0, sta, c, y_send.at[0, c], group_at(1))
    base, offset, tables = lag_groups(bands, quick_ref)
    for c in range(parts):
        own_column(0, c)
    for t in range(4):
        lag_tile(t, base, offset, tables, slow_ref, table)
    for c in range(parts):
        own_column(1, c)
    sides(0)
    for t in range(4, 8):
        lag_tile(t, base, offset, tables, slow_ref, table)
    far(0)
    several(0, sta, 1)
    sides(1)
    several(0, lax.rem(sta + 2, 8), 3)
    for d in range(4):
        by_mate(0, lax.rem(mate + 2 * d, 8))
    far(1)
    several(0, mate, 4)
    pack(0)
    for n in range(4):
        product(0, n)
    several(1, sta, 4)
    for d in range(4):
        by_mate(1, lax.rem(mate + 2 * d, 8))
    several(1, mate, 4)
    pack(1)
    for n in range(4):
        product(1, n)
    for copy in started:
        copy.wait_send()


def smem():
    return pl.BlockSpec(memory_space=pltpu.SMEM)


def vmem():
    return pl.BlockSpec(memory_space=pltpu.VMEM)


def body(records, fir_taps, band_bins, station_live, block_live):
    twiddle, second, slow, quick = constant_tables()
    f32, bf16 = jnp.float32, jnp.bfloat16
    x = jnp.transpose(records, (0, 2, 1, 3)).reshape(6, 4, -1)
    parts = 2
    dma = pltpu.SemaphoreType.DMA
    out = pl.pallas_call(
        functools.partial(whole_kernel, parts),
        out_shape=jax.ShapeDtypeStruct((288 * 16, 128), f32),
        in_specs=[smem(), smem(), smem(), smem(), pl.BlockSpec(memory_space=pl.ANY), vmem(), vmem(), vmem(), vmem()],
        out_specs=vmem(),
        scratch_shapes=[
            pltpu.VMEM((6, 4, 16384), bf16),
            pltpu.VMEM((WINDOW, FRAMES), f32),
            pltpu.VMEM((PADROWS * SPLIT, WINDOW), bf16),
            pltpu.VMEM((PADROWS * SPLIT, FRAMES), f32),
            pltpu.VMEM((ROWS * TILES, 1024), f32),
            pltpu.VMEM((ROWS * 16, 128), f32),
            pltpu.VMEM((1024, 512), bf16),
            pltpu.VMEM((ROWS * 16, 128), bf16),
            pltpu.VMEM((16, ROWS * 16, 128), bf16),
            pltpu.VMEM((1152 * TILES, 128), f32),
            pltpu.VMEM((576, 2048), bf16),
            pltpu.VMEM((2048, 1024), bf16),
            dma((6,)),
            dma((2, parts)),
            dma((2, 2, parts)),
            dma((2, parts)),
            dma((2, 4, parts)),
            dma((16, parts)),
        ],
        compiler_params=pltpu.CompilerParams(collective_id=0, has_side_effects=True, vmem_limit_bytes=VMEM_LIMIT),
        name="whole",
    )(jnp.transpose(band_bins), station_live, fir_taps, block_live, x, twiddle, second, slow, quick)
    out = out.reshape(288, 8, 2, 128)
    return jnp.transpose(out, (0, 2, 1, 3)).reshape(288, 2, 1024)


def solution(mesh):
    in_specs = (
        P(("section", "grp", "sta"), None, None, None),
        P(),
        P(),
        P(("section", "grp", "sta")),
        P(("section", "grp")),
    )
    out_specs = P("sta", ("section", "grp"), None)
    return jax.shard_map(body, mesh=mesh, in_specs=in_specs, out_specs=out_specs, check_vma=False)
```

time: 523 us -> 43.1 us (0.08)
  matrix products: 187 us -> 0 us
  other arithmetic: 160 us -> 0 us
  waiting for transfers between devices: 108 us -> 0 us
  local copies, waits for them, and re-layouts: 50.9 us -> 8.7 us
  Pallas kernels: 0 us -> 33.6 us
  between operations: 13.7 us -> 0.02 us
    dot_general x16 -> x0, matrix products: 187 us -> none  [the longest x4 97.4 us: inverse_advance(): jnp.dot(flattened, lag_table(frequency, parity, starts, block_width), pre...]
    another operation x10 -> x0, other arithmetic: 141 us -> none
    ppermute x2 -> x0, waiting for transfers between devices: 76.7 us -> none  [passed_along(): return lax.ppermute(block, axis, route)]
    pallas_call x0 -> x1, Pallas kernels: none -> 33.6 us  [body(): pl.pallas_call(functools.partial(whole_kernel, parts), out_shape=jax.Shap...]
    all_gather x1 -> x0, waiting for transfers between devices: 31.2 us -> none  [body(): gathered = lax.all_gather(local_spectra, 'sta', axis=0, tiled=True)]
    another operation x6 -> x0, local copies, waits for them, and re-layouts: 18.5 us -> none  [the longest x1 9.47 us: body(): arrived = jnp.stack(pieces, axis=1)]
    reduce_sum x1 -> x0, other arithmetic: 13 us -> none  [cross_spectra(): real_sum = jnp.sum(local_re * remote_re + local_im * remote_im, axis=4)]
    reshape x6 -> x0, local copies, waits for them, and re-layouts: 11.8 us -> none  [the longest x1 8.05 us: inverse(): flattened = spectra.reshape(row_count * block_count, depth)]
  transfers between devices with their start and end apart: 3 -> 0, of which waited for: 3 -> 0; matrix products, arithmetic and copies ran while one was open for 0% -> 0% of each run, Pallas kernels for 0% -> 0%
where the time goes in v2:
time: 43.1 us; the launch traced here: 42.3 us
  Pallas kernels  33.6 us (78%)
  local copies, waits for them, and re-layouts  8.7 us (20%)
    pallas_call x1, Pallas kernels, body(): pl.pallas_call(functools.partial(whole_kernel, parts), out_shape=jax.Shap...  33.6 us
    unnamed x19, local copies, waits for them, and re-layouts  8.7 us

profile of v2, /device:TPU:1, one launch (start us, length us, event | category | flops | bytes accessed | tf_op | source)
XLA Modules:
  0.0 42.3 jit_solution(6931219227149322476)
XLA Ops:
  0.0 0.0 copy-start
  0.0 1.1 %copy-done = bf16[2,4,3,16384]{3,1,2,0:T(4,128)(2,1)S(1)} copy-done((bf16[2,4,3,16384]{3,1,2,0:T(4,128)(2,1)S(1)}, bf16[2,4,3,16384]{3,1,2,0:T(4,128)(2,1)}, u32[]{:S(2)}) %copy-start) | copy-done | bytes 786456
  1.1 0.0 copy-start.1
  1.1 0.9 %copy-done.1 = f32[64,1024]{1,0:T(8,128)S(1)} copy-done((f32[64,1024]{1,0:T(8,128)S(1)}, f32[64,1024]{1,0:T(8,128)}, u32[]{:S(2)}) %copy-start.1) | copy-done | bytes 262168
  2.1 0.0 copy-start.2
  2.1 0.9 %copy-done.2 = f32[128,256]{1,0:T(8,128)S(1)} copy-done((f32[128,256]{1,0:T(8,128)S(1)}, f32[128,256]{1,0:T(8,128)}, u32[]{:S(2)}) %copy-start.2) | copy-done | bytes 131096
  3.0 0.0 copy-start.3
  3.0 0.9 %copy-done.3 = f32[256,64]{1,0:T(8,128)S(1)} copy-done((f32[256,64]{1,0:T(8,128)S(1)}, f32[256,64]{1,0:T(8,128)}, u32[]{:S(2)}) %copy-start.3) | copy-done | bytes 65560
  3.9 0.0 copy-start.4
  3.9 0.8 %copy-done.4 = f32[64,128]{1,0:T(8,128)S(1)} copy-done((f32[64,128]{1,0:T(8,128)S(1)}, f32[64,128]{1,0:T(8,128)}, u32[]{:S(2)}) %copy-start.4) | copy-done | bytes 32792
  4.7 0.0 copy-start.5
  4.7 0.7 %copy-done.5 = s32[4,2]{0,1:T(2,128)S(1)} copy-done((s32[4,2]{0,1:T(2,128)S(1)}, s32[4,2]{0,1:T(2,128)}, u32[]{:S(2)}) %copy-start.5) | copy-done | bytes 56
  5.3 0.0 copy-start.6
  5.3 0.7 %copy-done.6 = s32[2]{0:T(128)S(1)} copy-done((s32[2]{0:T(128)S(1)}, s32[2]{0:T(128)}, u32[]{:S(2)}) %copy-start.6) | copy-done | bytes 32
  6.0 0.0 copy-start.7
  6.0 0.7 %copy-done.7 = f32[64]{0:T(128)S(1)} copy-done((f32[64]{0:T(128)S(1)}, f32[64]{0:T(128)}, u32[]{:S(2)}) %copy-start.7) | copy-done | bytes 280
  6.6 0.0 copy-start.8
  6.6 0.7 %copy-done.8 = s32[2]{0:T(128)S(1)} copy-done((s32[2]{0:T(128)S(1)}, s32[2]{0:T(128)}, u32[]{:S(2)}) %copy-start.8) | copy-done | bytes 32
  7.3 33.6 %whole.1 = f32[4608,128]{1,0:T(8,128)S(1)} custom-call(s32[2,4]{1,0:T(2,128)S(1)} %bitcast.11, s32[2]{0:T(128)S(1)} %copy-done.6, f32[64]{0:T(128)S(1)} %copy-done.7, s32[2]{0:T(128)S(1)} %copy-done.8, bf16[6,4,16384]{2,1,0:T(4,128)(2,1)S(1)} %bitcast.10, f32[64,128]{1,0:T(8,128)S(1)} %copy-done.4, f32[256,64]{1,0:T(8,128)S(1)} %copy-done.3, ...), custom_call_target="tpu_custom_call" | custom-call | tf_op jit(solution)/shard_map/whole/pallas_call | solution.py:421
  40.9 1.4 %copy.12 = f32[288,2,1024]{2,1,0:T(2,128)} copy(f32[288,2,1024]{2,1,0:T(2,128)S(1)} %bitcast.9) | data formatting | bytes 4718592
Async XLA Ops:
  0.0 1.1 %copy-start = (bf16[2,4,3,16384]{3,1,2,0:T(4,128)(2,1)S(1)}, bf16[2,4,3,16384]{3,1,2,0:T(4,128)(2,1)}, u32[]{:S(2)}) copy-start(bf16[2,4,3,16384]{3,1,2,0:T(4,128)(2,1)} %param.9) | copy-start | bytes 2359300
  1.1 0.9 %copy-start.1 = (f32[64,1024]{1,0:T(8,128)S(1)}, f32[64,1024]{1,0:T(8,128)}, u32[]{:S(2)}) copy-start(f32[64,1024]{1,0:T(8,128)} %constant.10.clone.slow_ref) | copy-start | bytes 786436
  2.1 0.9 %copy-start.2 = (f32[128,256]{1,0:T(8,128)S(1)}, f32[128,256]{1,0:T(8,128)}, u32[]{:S(2)}) copy-start(f32[128,256]{1,0:T(8,128)} %constant.11.clone.quick_ref) | copy-start | bytes 393220
  3.0 0.9 %copy-start.3 = (f32[256,64]{1,0:T(8,128)S(1)}, f32[256,64]{1,0:T(8,128)}, u32[]{:S(2)}) copy-start(f32[256,64]{1,0:T(8,128)} %constant.9.clone.second_ref) | copy-start | bytes 196612
  3.9 0.8 %copy-start.4 = (f32[64,128]{1,0:T(8,128)S(1)}, f32[64,128]{1,0:T(8,128)}, u32[]{:S(2)}) copy-start(f32[64,128]{1,0:T(8,128)} %constant.8.clone.tw_ref) | copy-start | bytes 98308
  4.7 0.7 %copy-start.5 = (s32[4,2]{0,1:T(2,128)S(1)}, s32[4,2]{0,1:T(2,128)}, u32[]{:S(2)}) copy-start(s32[4,2]{0,1:T(2,128)} %param.11) | copy-start | bytes 100
  5.3 0.7 %copy-start.6 = (s32[2]{0:T(128)S(1)}, s32[2]{0:T(128)}, u32[]{:S(2)}) copy-start(s32[2]{0:T(128)} %live.1) | copy-start | bytes 28
  6.0 0.7 %copy-start.7 = (f32[64]{0:T(128)S(1)}, f32[64]{0:T(128)}, u32[]{:S(2)}) copy-start(f32[64]{0:T(128)} %taps.1) | copy-start | bytes 772
  6.6 0.7 %copy-start.8 = (s32[2]{0:T(128)S(1)}, s32[2]{0:T(128)}, u32[]{:S(2)}) copy-start(s32[2]{0:T(128)} %kept.1) | copy-start | bytes 28

commit v3 on v2

--- a/solution.py
+++ b/solution.py
@@ -247,8 +247,8 @@
                 cross[pl.ds(row + 576, 8, stride=1152), :] = im
 
 
-def whole_kernel(parts, bands, live, taps, kept, x_any, tw_ref, second_ref, slow_ref, quick_ref, out_ref,
-                 x_in, band_scr, lhs1, dec, lhs2, wide, w2, own_ref, got, cross, lhs, table,
+def whole_kernel(parts, bands_any, live_any, taps_any, kept_any, x_any, tw_any, second_any, slow_any, quick_any, out_ref,
+                 bands, live, taps, kept, tw_ref, second_ref, slow_ref, quick_ref, in_sem, x_in, band_scr, lhs1, dec, lhs2, wide, w2, own_ref, got, cross, lhs, table,
                  x_sem, y_send, x_send, f_send, m_send, recv):
     f32, bf16 = jnp.float32, jnp.bfloat16
     section, grp, sta = lax.axis_index("section"), lax.axis_index("grp"), lax.axis_index("sta")
@@ -265,13 +265,24 @@
         return (section, grp, s)
 
     barrier = pltpu.get_barrier_semaphore()
-    partners = [group_at(1), group_at(-1), near(mate), near(right), near(left_peer)]
+    partners = [group_at(1), group_at(-1), near(mate), near(right), near(left_peer), near(across)]
     for who in partners:
         pl.semaphore_signal(barrier, inc=1, device_id=who, device_id_type=MESH)
 
+    small = [
+        pltpu.make_async_copy(source, place, in_sem.at[n])
+        for n, (source, place) in enumerate([
+            (taps_any, taps), (bands_any, bands), (second_any, second_ref), (tw_any, tw_ref), (live_any, live),
+            (slow_any, slow_ref), (quick_any, quick_ref), (kept_any, kept),
+        ])
+    ]
+    for copy in small:
+        copy.start()
     fetches = [pltpu.make_async_copy(x_any.at[n], x_in.at[n], x_sem.at[n]) for n in range(6)]
     for fetch in fetches:
         fetch.start()
+    for copy in small:
+        copy.wait()
     weights = filter_weights(taps, band_scr)
     second_stage(bands, second_ref, w2)
     for fetch in fetches:
@@ -313,43 +324,40 @@
             recv_sem=recv.at[k * 8 + s, c], device_id=near(mate), device_id_type=MESH,
         ).wait_recv()
 
+    def block(k, s):
+        return got.at[k * 8 + s]
+
     def own_column(k, c):
         arrived(k, sta, c)
         if k == 0:
+            send(held(0, sta, c), 0, sta, c, f_send.at[0, c], near(across))
             send(held(0, sta, c), 1, sta, c, y_send.at[1, c], group_at(1))
         send(held(k, sta, c), k, sta, c, x_send.at[k, 0, c], near(right))
         send(held(k, sta, c), k, sta, c, x_send.at[k, 1, c], near(left_peer))
-        send(held(k, sta, c), k, sta, c, m_send.at[k, 0, c], near(mate))
-
-    def from_left(k, c):
-        arrived(k, left_peer, c)
-        if 2 * c < parts:
-            send(held(k, left_peer, c), k, left_peer, c, f_send.at[k, c], near(right))
-        send(held(k, left_peer, c), k, left_peer, c, m_send.at[k, 1, c], near(mate))
-
-    def from_right(k, c):
-        arrived(k, right, c)
-        if 2 * c >= parts:
-            send(held(k, right, c), k, right, c, f_send.at[k, c], near(left_peer))
-        send(held(k, right, c), k, right, c, m_send.at[k, 2, c], near(mate))
-
-    def from_across(k, c):
+
+    def far(k, c):
         arrived(k, across, c)
-        send(held(k, across, c), k, across, c, m_send.at[k, 3, c], near(mate))
-
-    def sides(k):
-        for c in range(parts):
-            from_left(k, c)
-            from_right(k, parts - 1 - c)
-
-    def far(k):
-        for c in range(parts // 2):
-            from_across(k, c)
-            from_across(k, parts // 2 + c)
-
-    def by_mate(k, s):
+        if k == 0:
+            send(held(0, across, c), 1, across, c, f_send.at[1, c], group_at(1))
+
+    def to_mate(k, s, n):
+        copy = pltpu.make_async_remote_copy(
+            src_ref=block(k, s), dst_ref=block(k, s), send_sem=m_send.at[k, n], recv_sem=recv.at[k * 8 + s, 0],
+            device_id=near(mate), device_id_type=MESH,
+        )
+        copy.start()
+        started.append(copy)
+
+    def side(k, s, n):
         for c in range(parts):
             arrived(k, s, c)
+        to_mate(k, s, n)
+
+    def by_mate(k, s):
+        pltpu.make_async_remote_copy(
+            src_ref=block(k, s), dst_ref=block(k, s), send_sem=m_send.at[k, 0], recv_sem=recv.at[k * 8 + s, 0],
+            device_id=near(mate), device_id_type=MESH,
+        ).wait_recv()
 
     def several(k, start, count):
         def one(n, carry):
@@ -373,26 +381,36 @@
     for c in range(parts):
         send(own_ref.at[pl.ds(c * rows, rows), :], 0, sta, c, y_send.at[0, c], group_at(1))
     base, offset, tables = lag_groups(bands, quick_ref)
+    for t in range(3):
+        lag_tile(t, base, offset, tables, slow_ref, table)
     for c in range(parts):
         own_column(0, c)
-    for t in range(4):
+    to_mate(0, sta, 0)
+    for t in range(3, 8):
         lag_tile(t, base, offset, tables, slow_ref, table)
     for c in range(parts):
         own_column(1, c)
-    sides(0)
-    for t in range(4, 8):
-        lag_tile(t, base, offset, tables, slow_ref, table)
-    far(0)
+    to_mate(1, sta, 0)
     several(0, sta, 1)
-    sides(1)
+    for c in range(parts):
+        far(0, c)
+    to_mate(0, across, 3)
+    side(0, left_peer, 1)
+    side(0, right, 2)
     several(0, lax.rem(sta + 2, 8), 3)
     for d in range(4):
         by_mate(0, lax.rem(mate + 2 * d, 8))
-    far(1)
     several(0, mate, 4)
     pack(0)
-    for n in range(4):
+    for n in range(2):
         product(0, n)
+    side(1, left_peer, 1)
+    side(1, right, 2)
+    for n in range(2, 4):
+        product(0, n)
+    for c in range(parts):
+        far(1, c)
+    to_mate(1, across, 3)
     several(1, sta, 4)
     for d in range(4):
         by_mate(1, lax.rem(mate + 2 * d, 8))
@@ -404,10 +422,6 @@
         copy.wait_send()
 
 
-def smem():
-    return pl.BlockSpec(memory_space=pltpu.SMEM)
-
-
 def vmem():
     return pl.BlockSpec(memory_space=pltpu.VMEM)
 
@@ -421,9 +435,18 @@
     out = pl.pallas_call(
         functools.partial(whole_kernel, parts),
         out_shape=jax.ShapeDtypeStruct((288 * 16, 128), f32),
-        in_specs=[smem(), smem(), smem(), smem(), pl.BlockSpec(memory_space=pl.ANY), vmem(), vmem(), vmem(), vmem()],
+        in_specs=[pl.BlockSpec(memory_space=pltpu.HBM)] * 9,
         out_specs=vmem(),
         scratch_shapes=[
+            pltpu.SMEM((2, 4), jnp.int32),
+            pltpu.SMEM((2,), jnp.int32),
+            pltpu.SMEM((64,), f32),
+            pltpu.SMEM((2,), jnp.int32),
+            pltpu.VMEM(twiddle.shape, f32),
+            pltpu.VMEM(second.shape, f32),
+            pltpu.VMEM(slow.shape, f32),
+            pltpu.VMEM(quick.shape, f32),
+            dma((8,)),
             pltpu.VMEM((6, 4, 16384), bf16),
             pltpu.VMEM((WINDOW, FRAMES), f32),
             pltpu.VMEM((PADROWS * SPLIT, WINDOW), bf16),
@@ -440,12 +463,18 @@
             dma((2, parts)),
             dma((2, 2, parts)),
             dma((2, parts)),
-            dma((2, 4, parts)),
+            dma((2, 4)),
             dma((16, parts)),
         ],
         compiler_params=pltpu.CompilerParams(collective_id=0, has_side_effects=True, vmem_limit_bytes=VMEM_LIMIT),
         name="whole",
-    )(jnp.transpose(band_bins), station_live, fir_taps, block_live, x, twiddle, second, slow, quick)
+    )(*[
+        pltpu.with_memory_space_constraint(operand, pltpu.HBM)
+        for operand in (
+            jnp.transpose(band_bins), station_live, fir_taps, block_live, x,
+            jnp.asarray(twiddle), jnp.asarray(second), jnp.asarray(slow), jnp.asarray(quick),
+        )
+    ])
     out = out.reshape(288, 8, 2, 128)
     return jnp.transpose(out, (0, 2, 1, 3)).reshape(288, 2, 1024)
 

time: 43.1 us -> 33.4 us (0.77); the launches traced: 42.3 us -> 33.3 us
  local copies, waits for them, and re-layouts: 8.7 us -> 1.41 us
  Pallas kernels: 33.6 us -> 31.8 us
    unnamed x19 -> x1, local copies, waits for them, and re-layouts: 8.7 us -> 1.41 us
    pallas_call x1, Pallas kernels: 33.6 us -> 31.8 us  [body(): pl.pallas_call(functools.partial(whole_kernel, parts), out_shape=jax.Shap...]
where the time goes in v3:
time: 33.4 us; the launch traced here: 33.3 us
  Pallas kernels  31.8 us (95%)
  local copies, waits for them, and re-layouts  1.41 us (4%)
    pallas_call x1, Pallas kernels, body(): pl.pallas_call(functools.partial(whole_kernel, parts), out_shape=jax.Shap...  31.8 us
    unnamed x1, local copies, waits for them, and re-layouts  1.41 us

profile of v3, /device:TPU:1, one launch (start us, length us, event | category | flops | bytes accessed | tf_op | source)
XLA Modules:
  0.0 33.3 jit_solution(13022702319462276421)
XLA Ops:
  0.0 31.8 %whole.1 = f32[4608,128]{1,0:T(8,128)S(1)} custom-call(s32[2,4]{1,0:T(2,128)} %bitcast.11, s32[2]{0:T(128)} %live_any.1, f32[64]{0:T(128)} %taps_any.1, s32[2]{0:T(128)} %kept_any.1, bf16[6,4,16384]{2,1,0:T(4,128)(2,1)} %bitcast.10, f32[64,128]{1,0:T(8,128)} %constant.8.clone.tw_any, f32[256,64]{1,0:T(8,128)} %constant.9.clone.second_any, ...), custom_call_target="tpu_custom_call" | custom-call | tf_op jit(solution)/shard_map/whole/pallas_call | solution.py:435
  31.9 1.4 %copy.12 = f32[288,2,1024]{2,1,0:T(2,128)} copy(f32[288,2,1024]{2,1,0:T(2,128)S(1)} %bitcast.9) | data formatting | bytes 4718592

commit v4 on v3

--- a/solution.py
+++ b/solution.py
@@ -15,6 +15,7 @@
 SPLIT = 32
 WINDOW = 640
 TILES = 8
+STEP = 1160
 MESH = pl.DeviceIdType.MESH
 VMEM_LIMIT = 40 * 1024 * 1024
 HIGHEST = lax.Precision.HIGHEST
@@ -243,8 +244,8 @@
                     re = pre if re is None else re + pre
                     im = pim if im is None else im + pim
                 row = k * 288 + ia * 48 + s * 6 + i2 * 3 + b
-                cross[pl.ds(row, 8, stride=1152), :] = re
-                cross[pl.ds(row + 576, 8, stride=1152), :] = im
+                cross[pl.ds(row, 8, stride=STEP), :] = re
+                cross[pl.ds(row + 576, 8, stride=STEP), :] = im
 
 
 def whole_kernel(parts, bands_any, live_any, taps_any, kept_any, x_any, tw_any, second_any, slow_any, quick_any, out_ref,
@@ -273,17 +274,20 @@
         pltpu.make_async_copy(source, place, in_sem.at[n])
         for n, (source, place) in enumerate([
             (taps_any, taps), (bands_any, bands), (second_any, second_ref), (tw_any, tw_ref), (live_any, live),
-            (slow_any, slow_ref), (quick_any, quick_ref), (kept_any, kept),
+            (quick_any, quick_ref), (slow_any, slow_ref), (kept_any, kept),
         ])
     ]
-    for copy in small:
+    for copy in small[:3]:
         copy.start()
     fetches = [pltpu.make_async_copy(x_any.at[n], x_in.at[n], x_sem.at[n]) for n in range(6)]
     for fetch in fetches:
         fetch.start()
-    for copy in small:
-        copy.wait()
+    for copy in small[3:]:
+        copy.start()
+    small[0].wait()
     weights = filter_weights(taps, band_scr)
+    small[1].wait()
+    small[2].wait()
     second_stage(bands, second_ref, w2)
     for fetch in fetches:
         fetch.wait()
@@ -298,6 +302,8 @@
             lhs1[rows, :] = x[:, 512 * j - 128:512 * j + 512]
     summed = jnp.dot(lhs1[...], weights, preferred_element_type=f32)
     dec[...] = (summed[:, :128] + summed[:, 128:]).astype(bf16).astype(f32)
+    small[3].wait()
+    small[4].wait()
     transform(dec, tw_ref, lhs2)
     y = jnp.dot(lhs2[...].astype(bf16), w2[...], preferred_element_type=f32)
     whiten_slots(bands, live, y, wide)
@@ -359,9 +365,12 @@
             device_id=near(mate), device_id_type=MESH,
         ).wait_recv()
 
-    def several(k, start, count):
+    def several(k, start, count, waiting=False):
         def one(n, carry):
-            cross_block(wide, got, cross, k, lax.rem(start + 2 * n, 8))
+            s = lax.rem(start + 2 * n, 8)
+            if waiting:
+                by_mate(k, s)
+            cross_block(wide, got, cross, k, s)
             return carry
         lax.fori_loop(0, count, one, 0)
 
@@ -370,7 +379,7 @@
         for t in range(TILES):
             for h in range(2):
                 column = 256 * t + 128 * h
-                lhs[rows, column:column + 128] = cross[pl.ds(1152 * t + 576 * h + 288 * k, 288), :].astype(bf16)
+                lhs[rows, column:column + 128] = cross[pl.ds(STEP * t + 576 * h + 288 * k, 288), :].astype(bf16)
 
     def product(k, n):
         part = jnp.dot(lhs[pl.ds(288 * k, 288), :], table[:, 256 * n:256 * n + 256], preferred_element_type=f32)
@@ -380,6 +389,8 @@
 
     for c in range(parts):
         send(own_ref.at[pl.ds(c * rows, rows), :], 0, sta, c, y_send.at[0, c], group_at(1))
+    for copy in small[5:]:
+        copy.wait()
     base, offset, tables = lag_groups(bands, quick_ref)
     for t in range(3):
         lag_tile(t, base, offset, tables, slow_ref, table)
@@ -402,24 +413,21 @@
         by_mate(0, lax.rem(mate + 2 * d, 8))
     several(0, mate, 4)
     pack(0)
-    for n in range(2):
+    for n in range(0, 4):
         product(0, n)
     side(1, left_peer, 1)
     side(1, right, 2)
-    for n in range(2, 4):
-        product(0, n)
     for c in range(parts):
         far(1, c)
     to_mate(1, across, 3)
     several(1, sta, 4)
-    for d in range(4):
-        by_mate(1, lax.rem(mate + 2 * d, 8))
-    several(1, mate, 4)
+    several(1, lax.rem(mate + 6, 8), 3, True)
+    for copy in started:
+        copy.wait_send()
+    several(1, lax.rem(mate + 4, 8), 1, True)
     pack(1)
     for n in range(4):
         product(1, n)
-    for copy in started:
-        copy.wait_send()
 
 
 def vmem():
@@ -456,7 +464,7 @@
             pltpu.VMEM((1024, 512), bf16),
             pltpu.VMEM((ROWS * 16, 128), bf16),
             pltpu.VMEM((16, ROWS * 16, 128), bf16),
-            pltpu.VMEM((1152 * TILES, 128), f32),
+            pltpu.VMEM((STEP * TILES, 128), f32),
             pltpu.VMEM((576, 2048), bf16),
             pltpu.VMEM((2048, 1024), bf16),
             dma((6,)),

time: 33.4 us -> 31.4 us (0.940)
  Pallas kernels: 31.8 us -> 29.9 us
    pallas_call x1, Pallas kernels: 31.8 us -> 29.9 us  [body(): pl.pallas_call(functools.partial(whole_kernel, parts), out_shape=jax.Shap...]
where the time goes in v4:
time: 31.4 us; the launch traced here: 31.3 us
  Pallas kernels  29.9 us (95%)
  local copies, waits for them, and re-layouts  1.41 us (4%)
    pallas_call x1, Pallas kernels, body(): pl.pallas_call(functools.partial(whole_kernel, parts), out_shape=jax.Shap...  29.9 us
    unnamed x1, local copies, waits for them, and re-layouts  1.41 us

profile of v4, /device:TPU:1, one launch (start us, length us, event | category | flops | bytes accessed | tf_op | source)
XLA Modules:
  0.0 31.3 jit_solution(11468479004562788830)
XLA Ops:
  0.0 29.9 %whole.1 = f32[4608,128]{1,0:T(8,128)S(1)} custom-call(s32[2,4]{1,0:T(2,128)} %bitcast.11, s32[2]{0:T(128)} %live_any.1, f32[64]{0:T(128)} %taps_any.1, s32[2]{0:T(128)} %kept_any.1, bf16[6,4,16384]{2,1,0:T(4,128)(2,1)} %bitcast.10, f32[64,128]{1,0:T(8,128)} %constant.8.clone.tw_any, f32[256,64]{1,0:T(8,128)} %constant.9.clone.second_any, ...), custom_call_target="tpu_custom_call" | custom-call | tf_op jit(solution)/shard_map/whole/pallas_call | solution.py:443
  29.9 1.4 %copy.12 = f32[288,2,1024]{2,1,0:T(2,128)} copy(f32[288,2,1024]{2,1,0:T(2,128)S(1)} %bitcast.9) | data formatting | bytes 4718592

commit v5 on v4

--- a/solution.py
+++ b/solution.py
@@ -10,7 +10,6 @@
 from jax.sharding import PartitionSpec as P
 
 ROWS = 24
-PADROWS = 32
 FRAMES = 128
 SPLIT = 32
 WINDOW = 640
@@ -123,27 +122,23 @@
             w2[under, im] = c.astype(bf16)
 
 
-def transform(dec, tw_ref, lhs2):
-    def one(chunk, carry):
-        values = [dec[pl.ds(PADROWS * j + 8 * chunk, 8), :] for j in range(SPLIT)]
-        freq = real_fft(values)
-        for k1 in range(32):
-            ar, ai = freq[k1] if k1 <= 16 else freq[32 - k1]
-            c = tw_ref[pl.ds(k1, 1), :]
-            s = tw_ref[pl.ds(32 + k1, 1), :]
-            if ai is None:
-                br, bi = ar * c, ar * s
-            elif k1 <= 16:
-                br, bi = ar * c - ai * s, ar * s + ai * c
-            else:
-                br, bi = ar * c + ai * s, ar * s - ai * c
-            rows = pl.ds((k1 // 4) * ROWS + 8 * chunk, 8)
-            column = (k1 % 4) * 256
-            lhs2[rows, column:column + 128] = br
-            lhs2[rows, column + 128:column + 256] = bi
-        return carry
-
-    lax.fori_loop(0, 3, one, 0)
+def transform(chunk, dec, tw_ref, lhs2):
+    values = [dec[pl.ds(256 * chunk + 8 * j, 8), :] for j in range(SPLIT)]
+    freq = real_fft(values)
+    for k1 in range(32):
+        ar, ai = freq[k1] if k1 <= 16 else freq[32 - k1]
+        c = tw_ref[pl.ds(k1, 1), :]
+        s = tw_ref[pl.ds(32 + k1, 1), :]
+        if ai is None:
+            br, bi = ar * c, ar * s
+        elif k1 <= 16:
+            br, bi = ar * c - ai * s, ar * s + ai * c
+        else:
+            br, bi = ar * c + ai * s, ar * s - ai * c
+        rows = pl.ds((k1 // 4) * ROWS + 8 * chunk, 8)
+        column = (k1 % 4) * 256
+        lhs2[rows, column:column + 128] = br
+        lhs2[rows, column + 128:column + 256] = bi
 
 
 def whiten_slots(bands, live, y, wide):
@@ -289,22 +284,21 @@
     small[1].wait()
     small[2].wait()
     second_stage(bands, second_ref, w2)
-    for fetch in fetches:
-        fetch.wait()
-    x = x_in[...].reshape(ROWS, -1)
-    x = jnp.concatenate([x, jnp.zeros((PADROWS - ROWS, x.shape[1]), bf16)], axis=0)
-    for j in range(SPLIT):
-        rows = pl.ds(PADROWS * j, PADROWS)
-        if j == 0:
-            lhs1[rows, 0:128] = jnp.zeros((PADROWS, 128), bf16)
-            lhs1[rows, 128:] = x[:, 0:512]
-        else:
-            lhs1[rows, :] = x[:, 512 * j - 128:512 * j + 512]
-    summed = jnp.dot(lhs1[...], weights, preferred_element_type=f32)
-    dec[...] = (summed[:, :128] + summed[:, 128:]).astype(bf16).astype(f32)
     small[3].wait()
     small[4].wait()
-    transform(dec, tw_ref, lhs2)
+    for chunk in range(3):
+        fetches[2 * chunk].wait()
+        fetches[2 * chunk + 1].wait()
+        x = x_in[2 * chunk:2 * chunk + 2].reshape(8, -1)
+        edge = jnp.concatenate([jnp.zeros((8, 128), bf16), x[:, 0:512]], axis=1)
+        first = 256 * chunk
+        for j in range(0, SPLIT, 2):
+            head = edge if j == 0 else x[:, 512 * j - 128:512 * j + 512]
+            both = jnp.concatenate([head, x[:, 512 * j + 384:512 * j + 1024]], axis=0)
+            lhs1[pl.ds(first + 8 * j, 16), :] = both
+        summed = jnp.dot(lhs1[pl.ds(first, 256), :], weights, preferred_element_type=f32)
+        dec[pl.ds(first, 256), :] = (summed[:, :128] + summed[:, 128:]).astype(bf16).astype(f32)
+        transform(chunk, dec, tw_ref, lhs2)
     y = jnp.dot(lhs2[...].astype(bf16), w2[...], preferred_element_type=f32)
     whiten_slots(bands, live, y, wide)
     own_ref[...] = wide[...].astype(bf16)
@@ -338,25 +332,34 @@
         if k == 0:
             send(held(0, sta, c), 0, sta, c, f_send.at[0, c], near(across))
             send(held(0, sta, c), 1, sta, c, y_send.at[1, c], group_at(1))
-        send(held(k, sta, c), k, sta, c, x_send.at[k, 0, c], near(right))
-        send(held(k, sta, c), k, sta, c, x_send.at[k, 1, c], near(left_peer))
+            send(held(k, sta, c), k, sta, c, x_send.at[k, 0, c], near(right))
+            send(held(k, sta, c), k, sta, c, x_send.at[k, 1, c], near(left_peer))
+        elif c == parts - 1:
+            to_peer(1, sta, x_send.at[1, 0, 0], near(right))
+            to_peer(1, sta, x_send.at[1, 1, 0], near(left_peer))
 
     def far(k, c):
         arrived(k, across, c)
         if k == 0:
             send(held(0, across, c), 1, across, c, f_send.at[1, c], group_at(1))
 
-    def to_mate(k, s, n):
+    def to_peer(k, s, sem, who):
         copy = pltpu.make_async_remote_copy(
-            src_ref=block(k, s), dst_ref=block(k, s), send_sem=m_send.at[k, n], recv_sem=recv.at[k * 8 + s, 0],
-            device_id=near(mate), device_id_type=MESH,
+            src_ref=block(k, s), dst_ref=block(k, s), send_sem=sem, recv_sem=recv.at[k * 8 + s, 0],
+            device_id=who, device_id_type=MESH,
         )
         copy.start()
         started.append(copy)
 
+    def to_mate(k, s, n):
+        to_peer(k, s, m_send.at[k, n], near(mate))
+
     def side(k, s, n):
-        for c in range(parts):
-            arrived(k, s, c)
+        if k == 0:
+            for c in range(parts):
+                arrived(k, s, c)
+        else:
+            by_mate(k, s)
         to_mate(k, s, n)
 
     def by_mate(k, s):
@@ -364,6 +367,9 @@
             src_ref=block(k, s), dst_ref=block(k, s), send_sem=m_send.at[k, 0], recv_sem=recv.at[k * 8 + s, 0],
             device_id=near(mate), device_id_type=MESH,
         ).wait_recv()
+
+    def one_block(k, s):
+        cross_block(wide, got, cross, k, s)
 
     def several(k, start, count, waiting=False):
         def one(n, carry):
@@ -392,13 +398,11 @@
     for copy in small[5:]:
         copy.wait()
     base, offset, tables = lag_groups(bands, quick_ref)
-    for t in range(3):
+    for t in range(8):
         lag_tile(t, base, offset, tables, slow_ref, table)
     for c in range(parts):
         own_column(0, c)
     to_mate(0, sta, 0)
-    for t in range(3, 8):
-        lag_tile(t, base, offset, tables, slow_ref, table)
     for c in range(parts):
         own_column(1, c)
     to_mate(1, sta, 0)
@@ -413,14 +417,19 @@
         by_mate(0, lax.rem(mate + 2 * d, 8))
     several(0, mate, 4)
     pack(0)
-    for n in range(0, 4):
+    for n in range(2):
         product(0, n)
     side(1, left_peer, 1)
     side(1, right, 2)
     for c in range(parts):
         far(1, c)
     to_mate(1, across, 3)
-    several(1, sta, 4)
+    product(0, 2)
+    one_block(1, sta)
+    one_block(1, left_peer)
+    product(0, 3)
+    one_block(1, right)
+    one_block(1, across)
     several(1, lax.rem(mate + 6, 8), 3, True)
     for copy in started:
         copy.wait_send()
@@ -457,8 +466,8 @@
             dma((8,)),
             pltpu.VMEM((6, 4, 16384), bf16),
             pltpu.VMEM((WINDOW, FRAMES), f32),
-            pltpu.VMEM((PADROWS * SPLIT, WINDOW), bf16),
-            pltpu.VMEM((PADROWS * SPLIT, FRAMES), f32),
+            pltpu.VMEM((ROWS * SPLIT, WINDOW), bf16),
+            pltpu.VMEM((ROWS * SPLIT, FRAMES), f32),
             pltpu.VMEM((ROWS * TILES, 1024), f32),
             pltpu.VMEM((ROWS * 16, 128), f32),
             pltpu.VMEM((1024, 512), bf16),

time: 31.4 us -> 31 us (0.987)
  Pallas kernels: 29.9 us -> 29.5 us
    pallas_call x1, Pallas kernels: 29.9 us -> 29.5 us  [body(): pl.pallas_call(functools.partial(whole_kernel, parts), out_shape=jax.Shap...]
where the time goes in v5:
time: 31 us; the launch traced here: 30.9 us
  Pallas kernels  29.5 us (95%)
  local copies, waits for them, and re-layouts  1.41 us (5%)
    pallas_call x1, Pallas kernels, body(): pl.pallas_call(functools.partial(whole_kernel, parts), out_shape=jax.Shap...  29.5 us
    unnamed x1, local copies, waits for them, and re-layouts  1.41 us

profile of v5, /device:TPU:1, one launch (start us, length us, event | category | flops | bytes accessed | tf_op | source)
XLA Modules:
  0.0 30.9 jit_solution(17780345144799048731)
XLA Ops:
  0.0 29.5 %whole.1 = f32[4608,128]{1,0:T(8,128)S(1)} custom-call(s32[2,4]{1,0:T(2,128)} %bitcast.11, s32[2]{0:T(128)} %live_any.1, f32[64]{0:T(128)} %taps_any.1, s32[2]{0:T(128)} %kept_any.1, bf16[6,4,16384]{2,1,0:T(4,128)(2,1)} %bitcast.10, f32[64,128]{1,0:T(8,128)} %constant.8.clone.tw_any, f32[256,64]{1,0:T(8,128)} %constant.9.clone.second_any, ...), custom_call_target="tpu_custom_call" | custom-call | tf_op jit(solution)/shard_map/whole/pallas_call | solution.py:452
  29.5 1.4 %copy.12 = f32[288,2,1024]{2,1,0:T(2,128)} copy(f32[288,2,1024]{2,1,0:T(2,128)S(1)} %bitcast.9) | data formatting | bytes 4718592

commit v6 on v5

--- a/solution.py
+++ b/solution.py
@@ -260,11 +260,6 @@
     def near(s):
         return (section, grp, s)
 
-    barrier = pltpu.get_barrier_semaphore()
-    partners = [group_at(1), group_at(-1), near(mate), near(right), near(left_peer), near(across)]
-    for who in partners:
-        pl.semaphore_signal(barrier, inc=1, device_id=who, device_id_type=MESH)
-
     small = [
         pltpu.make_async_copy(source, place, in_sem.at[n])
         for n, (source, place) in enumerate([
@@ -279,6 +274,11 @@
         fetch.start()
     for copy in small[3:]:
         copy.start()
+    barrier = pltpu.get_barrier_semaphore()
+    partners = [group_at(1), group_at(-1), near(mate), near(right), near(left_peer), near(across)]
+    for who in partners:
+        pl.semaphore_signal(barrier, inc=1, device_id=who, device_id_type=MESH)
+
     small[0].wait()
     weights = filter_weights(taps, band_scr)
     small[1].wait()
@@ -372,13 +372,11 @@
         cross_block(wide, got, cross, k, s)
 
     def several(k, start, count, waiting=False):
-        def one(n, carry):
+        for n in range(count):
             s = lax.rem(start + 2 * n, 8)
             if waiting:
                 by_mate(k, s)
             cross_block(wide, got, cross, k, s)
-            return carry
-        lax.fori_loop(0, count, one, 0)
 
     def pack(k):
         rows = pl.ds(288 * k, 288)

time: 31 us -> 31 us (level)
  no operation moved by 1% of the time
where the time goes in v6:
time: 31 us; the launch traced here: 30.9 us
  Pallas kernels  29.5 us (95%)
  local copies, waits for them, and re-layouts  1.41 us (5%)
    pallas_call x1, Pallas kernels, body(): pl.pallas_call(functools.partial(whole_kernel, parts), out_shape=jax.Shap...  29.5 us
    unnamed x1, local copies, waits for them, and re-layouts  1.41 us

profile of v6, /device:TPU:1, one launch (start us, length us, event | category | flops | bytes accessed | tf_op | source)
XLA Modules:
  0.0 30.9 jit_solution(13660076111145423986)
XLA Ops:
  0.0 29.5 %whole.1 = f32[4608,128]{1,0:T(8,128)S(1)} custom-call(s32[2,4]{1,0:T(2,128)} %bitcast.11, s32[2]{0:T(128)} %live_any.1, f32[64]{0:T(128)} %taps_any.1, s32[2]{0:T(128)} %kept_any.1, bf16[6,4,16384]{2,1,0:T(4,128)(2,1)} %bitcast.10, f32[64,128]{1,0:T(8,128)} %constant.8.clone.tw_any, f32[256,64]{1,0:T(8,128)} %constant.9.clone.second_any, ...), custom_call_target="tpu_custom_call" | custom-call | tf_op jit(solution)/shard_map/whole/pallas_call | solution.py:450
  29.5 1.4 %copy.12 = f32[288,2,1024]{2,1,0:T(2,128)} copy(f32[288,2,1024]{2,1,0:T(2,128)S(1)} %bitcast.9) | data formatting | bytes 4718592

commit v7 on v6

--- a/solution.py
+++ b/solution.py
@@ -330,8 +330,8 @@
     def own_column(k, c):
         arrived(k, sta, c)
         if k == 0:
+            send(held(0, sta, c), 1, sta, c, y_send.at[1, c], group_at(1))
             send(held(0, sta, c), 0, sta, c, f_send.at[0, c], near(across))
-            send(held(0, sta, c), 1, sta, c, y_send.at[1, c], group_at(1))
             send(held(k, sta, c), k, sta, c, x_send.at[k, 0, c], near(right))
             send(held(k, sta, c), k, sta, c, x_send.at[k, 1, c], near(left_peer))
         elif c == parts - 1:

time: 31 us -> 31 us (level)
  no operation moved by 1% of the time
where the time goes in v7:
time: 31 us; the launch traced here: 30.9 us
  Pallas kernels  29.5 us (95%)
  local copies, waits for them, and re-layouts  1.41 us (5%)
    pallas_call x1, Pallas kernels, body(): pl.pallas_call(functools.partial(whole_kernel, parts), out_shape=jax.Shap...  29.5 us
    unnamed x1, local copies, waits for them, and re-layouts  1.41 us

profile of v7, /device:TPU:1, one launch (start us, length us, event | category | flops | bytes accessed | tf_op | source)
XLA Modules:
  0.0 30.9 jit_solution(4581130116864605053)
XLA Ops:
  0.0 29.5 %whole.1 = f32[4608,128]{1,0:T(8,128)S(1)} custom-call(s32[2,4]{1,0:T(2,128)} %bitcast.11, s32[2]{0:T(128)} %live_any.1, f32[64]{0:T(128)} %taps_any.1, s32[2]{0:T(128)} %kept_any.1, bf16[6,4,16384]{2,1,0:T(4,128)(2,1)} %bitcast.10, f32[64,128]{1,0:T(8,128)} %constant.8.clone.tw_any, f32[256,64]{1,0:T(8,128)} %constant.9.clone.second_any, ...), custom_call_target="tpu_custom_call" | custom-call | tf_op jit(solution)/shard_map/whole/pallas_call | solution.py:450
  29.5 1.4 %copy.12 = f32[288,2,1024]{2,1,0:T(2,128)} copy(f32[288,2,1024]{2,1,0:T(2,128)S(1)} %bitcast.9) | data formatting | bytes 4718592
